TPU v7x, 128 devices: a whole 4x4x4 slice. The times are simulated.
128 devices in a mesh: slab: 16 (over z, x), cross: 8 (over y, core).
Axes of the slice: x: 4, y: 4, z: 4, core: 2. Of those that a mesh axis runs over, the one named last changes fastest.
Arguments:
- fields: bfloat16 [256, 64, 257, 128], P('slab', 'cross'), may hold values from -1.5 to 1.5
- strain_map: bfloat16 [162, 108], replicated, may hold values from -0.625 to 0.625
- quad_weight: float32 [27, 524288], P(None, ('slab', 'cross')), may hold values from 0.25 to 4
- param: float32 [1048576], P(('slab', 'cross')), may hold values from -3 to 3
- elem_order: int32 [524288], P(('slab', 'cross')), may hold values from 0 to 4095, as said below
- send_elem: int32 [128, 128, 64], P(('slab', 'cross')), may hold values from 0 to 4095, as said below
- send_count: int32 [128, 128], P(('slab', 'cross')), may hold values from 0 to 64, as said below
- recv_cell: int32 [128, 128, 64], P(('slab', 'cross')), may hold values from 0 to 8191
Outputs:
- hessian_terms: float32 [16, 8, 1048576], P(None, None, ('slab', 'cross'))
Inputs may be any that keep to these rules, and one draw needn't show every extreme that they name: `elem_order`: each device's 4096 entries are a permutation of its local element positions. `send_elem`: the live slots of one sender, over all owners, name each of its 4096 elements exactly once; slots at or past a block's count hold arbitrary element numbers. `send_count`: each sender's counts sum to 4096; one owner gets 64 live slots from every sender. `recv_cell`: slots at or past the sender's count carry nothing.
All inputs are finite; a program needn't handle non-finite values.
Results may differ from a plain program's by a relative error of at most 0.0003.
Values may be sent and summed in bfloat16 or wider, within the bound.
No kernel may reach another device: no remote copies, remote signals or barrier semaphores. Data moves between devices by JAX's collectives and lax.ppermute only.
A program may use at most 128 MiB of HBM per device.

v0:
```python
import math

import jax
import jax.numpy as jnp
from jax import lax
from jax.sharding import PartitionSpec as P


def passed_along(value, axis, steps):
    count = lax.axis_size(axis)
    initial, last = (max(0, -steps), min(count, count - steps))
    return lax.ppermute(value, axis, [(source, source + steps) for source in range(initial, last)])


def gauss_basis():
    spread = math.sqrt(0.15)
    places = jnp.array([0.5 - spread, 0.5, 0.5 + spread], jnp.float32)
    points = jnp.arange(27, dtype=jnp.int32)
    coeffs = jnp.arange(8, dtype=jnp.int32)
    result = jnp.ones((27, 8), jnp.float32)
    for point_axis, coeff_axis in (
        (points // 9, coeffs // 4),
        (points // 3 % 3, coeffs // 2 % 2),
        (points % 3, coeffs % 2),
    ):
        where_x = places[point_axis][:, None]
        result = result * jnp.where(coeff_axis[None, :] == 1, where_x, 1.0 - where_x)
    return result


def structured_partials(extended, weights_struct, strain_map, x_elems, y_elems, z_elems):
    channels = extended.shape[3]
    rows_out = strain_map.shape[0]
    strain_table = strain_map.reshape(rows_out, 27, 4)
    basis = gauss_basis()
    row_elems = y_elems * z_elems

    def one_row(row_index):
        planes = lax.dynamic_slice_in_dim(extended, 2 * row_index, 3, 0)
        corner_list = []
        for node in range(27):
            first = node // 9
            second = node // 3 % 3
            third = node % 3
            corner_list.append(
                planes[
                    first,
                    second : second + 2 * y_elems - 1 : 2,
                    third : third + 2 * z_elems - 1 : 2,
                ]
            )
        stacked = jnp.stack(corner_list, axis=0).reshape(27, row_elems, 2, 4, channels // 8)
        strain = jnp.einsum(
            "qnc,nefcd->fdqe", strain_table, stacked, preferred_element_type=jnp.float32
        )
        product = strain[0] * strain[1]
        product = jnp.sum(product.reshape(product.shape[0], 27, 6, row_elems), axis=2)
        weights_row = lax.dynamic_slice_in_dim(weights_struct, row_index * row_elems, row_elems, 1)
        weighted = product * weights_row[None, :, :]
        return jnp.einsum("dge,gt->edt", weighted, basis, precision=lax.Precision.HIGHEST)

    per_row = lax.map(one_row, jnp.arange(x_elems, dtype=jnp.int32))
    return per_row.reshape(x_elems * row_elems, -1)


def on_device(fields, strain_map, quad_weight, param, elem_order, send_elem, send_count, recv_cell):
    next_face = passed_along(fields[0:1], "slab", -1)
    grown = jnp.concatenate([fields, next_face], axis=0)
    next_side = passed_along(grown[:, 0:1], "cross", -1)
    extended = jnp.concatenate([grown, next_side], axis=1)
    x_elems = fields.shape[0] // 2
    y_elems = fields.shape[1] // 2
    z_elems = (fields.shape[2] - 1) // 2
    elem_count = elem_order.shape[0]
    inverse = (
        jnp.zeros((elem_count,), jnp.int32)
        .at[elem_order]
        .set(jnp.arange(elem_count, dtype=jnp.int32))
    )
    weights_struct = quad_weight[:, inverse]
    partial_rows = structured_partials(
        extended, weights_struct, strain_map, x_elems, y_elems, z_elems
    )
    lanes = partial_rows.shape[1]
    capacity = send_elem.shape[2]
    slot_ids = jnp.arange(capacity, dtype=jnp.int32)
    live_slots = slot_ids[None, :] < send_count[0][:, None]
    outgoing = partial_rows[elem_order[send_elem[0]]]
    outgoing = jnp.where(live_slots[:, :, None], outgoing, 0.0)
    incoming = lax.all_to_all(outgoing, ("slab", "cross"), split_axis=0, concat_axis=0, tiled=True)
    flowing = incoming.reshape(-1, lanes)
    cell_ids = recv_cell[0].reshape(-1)
    gradient = jnp.zeros((param.shape[0], lanes), jnp.float32).at[cell_ids].add(flowing)
    terms = gradient.T.reshape(lanes // 8, 8, param.shape[0])
    return terms * jnp.exp(param)[None, None, :]


def solution(mesh):
    return jax.shard_map(
        on_device,
        mesh=mesh,
        in_specs=(
            P("slab", "cross", None, None),
            P(),
            P(None, ("slab", "cross")),
            P(("slab", "cross")),
            P(("slab", "cross")),
            P(("slab", "cross"), None, None),
            P(("slab", "cross"), None),
            P(("slab", "cross"), None, None),
        ),
        out_specs=P(None, None, ("slab", "cross")),
        check_vma=False,
    )
```

profile of v0, /device:TPU:1, one launch (start us, length us, event | category | flops | bytes accessed | tf_op | source)
XLA Modules:
  0.0 784.0 jit_solution(7297556317694122921)
XLA Ops:
  2.4 8.6 %copy_dynamic-update-slice_fusion = bf16[17,8,257,128]{3,2,1,0:T(8,128)(2,1)} fusion(bf16[16,8,257,128]{3,1,2,0:T(8,128)(2,1)} %param.11), kind=kLoop, calls=%fused_computation.59 | loop fusion | bytes 17072128
  11.1 15.5 %scatter_custom_fusion = s32[4096]{0:T(1024)S(1)} fusion(s32[4096]{0:T(1024)S(1)} %compare_select_fusion.4, s32[4096]{0:T(1024)S(1)} %iota.42, s32[]{:T(128)} %constant.102.clone.1), kind=kCustom, calls=%fused_computation.74 | custom fusion | bytes 16388 | tf_op jit(solution)/shard_map/scatter | solution.py:78
  26.7 1.7 copy.49
  28.4 14.2 %gather_fusion = f32[4096,27]{1,0:T(8,128)} fusion(f32[27,4096]{0,1:T(8,128)S(1)} %copy.49, s32[4096]{0:T(1024)S(1)} %fusion.26), kind=kCustom, calls=%fused_computation | custom fusion | bytes 901120 | tf_op jit(solution)/shard_map/gather | solution.py:80
  42.6 3.0 copy.52
  46.5 45.5 %gather_fusion.1 = s32[8192]{0:T(1024)S(1)} fusion(s32[4096]{0:T(1024)S(1)} %copy-done, s32[8192]{0:T(1024)S(1)} %broadcast_clamp_fusion), kind=kCustom, calls=%fused_computation.1 | custom fusion | bytes 98304 | tf_op jit(solution)/shard_map/gather | solution.py:88
  94.4 3.3 collective-permute-start.1
  101.9 10.7 %collective-permute-done.1 = bf16[17,1,257,128]{3,2,1,0:T(8,128)(2,1)S(1)} collective-permute-done((bf16[17,1,257,128]{3,2,1,0:T(8,128)(2,1)S(1)}, bf16[17,1,257,128]{3,2,1,0:T(8,128)(2,1)S(1)}, u32[]{:S(2)}, u32[]{:S(2)}) %collective-permute-start.1) | collective-permute-done | bytes 1118496 | tf_op jit(solution)/shard_map/ppermute | solution.py:12
  112.6 9.3 %pad_maximum_fusion = bf16[17,9,257,128]{3,2,1,0:T(8,128)(2,1)} fusion(bf16[17,1,257,128]{3,2,1,0:T(8,128)(2,1)S(1)} %collective-permute-done.1, bf16[17,8,257,128]{3,2,1,0:T(8,128)(2,1)} %copy_dynamic-update-slice_fusion.1), kind=kLoop, calls=%fused_computation.58 | loop fusion | flops 5033088 | bytes 20132352 | tf_op jit(solution)/shard_map/concatenate | solution.py:70
  122.4 500.8 %while.11 = (s32[]{:T(128)}, f32[8,512,16,8]{1,0,3,2:T(8,128)}, s32[8]{0:T(128)}, bf16[17,9,257,128]{3,2,1,0:T(8,128)(2,1)}, bf16[162,27,4]{0,1,2:T(8,128)(2,1)}...) while((s32[]{:T(128)}, f32[8,512,16,8]{1,0,3,2:T(8,128)}, ...), condition=%wide.region_3.4_spmd.clone, body=%wide.region_1.3_spmd.clone.sunk | while | flops 597197888 | bytes 82925096 | solution.py:62
  124.1 1.6 constant_dynamic-slice_fusion.4
  155.7 5.6 reshape.421
  161.3 4.0 fusion.46
  166.6 5.5 copy.158
  172.2 3.3 reduce_sum.11
  178.7 6.3 dynamic_update_slice.6
  186.8 1.6 constant_dynamic-slice_fusion.4
  218.3 5.6 reshape.421
  223.9 4.0 fusion.46
  229.2 5.5 copy.158
  234.8 3.3 reduce_sum.11
  241.3 6.3 dynamic_update_slice.6
  249.4 1.6 constant_dynamic-slice_fusion.4
  280.9 5.6 reshape.421
  286.5 4.0 fusion.46
  291.8 5.5 copy.158
  297.4 3.3 reduce_sum.11
  303.9 6.3 dynamic_update_slice.6
  343.5 5.6 reshape.421
  349.1 4.0 fusion.46
  354.4 5.5 copy.158
  360.0 3.3 reduce_sum.11
  366.5 6.3 dynamic_update_slice.6
  374.6 1.6 constant_dynamic-slice_fusion.4
  406.1 5.6 reshape.421
  411.7 4.0 fusion.46
  417.0 5.5 copy.158
  422.6 3.3 reduce_sum.11
  429.1 6.3 dynamic_update_slice.6
  437.2 1.6 constant_dynamic-slice_fusion.4
  468.7 5.6 reshape.421
  474.3 4.0 fusion.46
  479.7 5.5 copy.158
  485.2 3.3 reduce_sum.11
  491.7 6.3 dynamic_update_slice.6
  531.3 5.6 reshape.421
  536.9 4.0 fusion.46
  542.3 5.5 copy.158
  547.8 3.3 reduce_sum.11
  554.3 6.3 dynamic_update_slice.6
  593.9 5.6 reshape.421
  599.5 4.0 fusion.46
  604.9 5.5 copy.158
  610.4 3.3 reduce_sum.11
  616.9 6.3 dynamic_update_slice.6
  623.2 4.6 copy.89
  627.8 1.9 copy.55
  629.7 28.0 %gather_fusion.2 = f32[8192,128]{1,0:T(8,128)} fusion(f32[4096,128]{1,0:T(8,128)S(1)} %copy.55, s32[8192]{0:T(1024)S(1)} %copy-done.1), kind=kCustom, calls=%fused_computation.2 | custom fusion | bytes 8421376 | tf_op jit(solution)/shard_map/gather | solution.py:88
  657.7 5.2 broadcast_select_fusion
  662.9 11.5 %all-to-all-start = ((f32[128,64,128]{2,1,0:T(8,128)}), f32[128,64,128]{2,1,0:T(8,128)}, u32[]{:S(2)}, u32[]{:S(2)}) async-start(f32[128,64,128]{2,1,0:T(8,128)} %broadcast_select_fusion), calls=%async_computation | async-start | bytes 8388608 | tf_op jit(solution)/shard_map/all_to_all | solution.py:90
  674.7 52.5 %all-to-all-done = f32[128,64,128]{2,1,0:T(8,128)} async-done(((f32[128,64,128]{2,1,0:T(8,128)}), f32[128,64,128]{2,1,0:T(8,128)}, u32[]{:S(2)}, u32[]{:S(2)}) %all-to-all-start) | async-done | bytes 4194336 | tf_op jit(solution)/shard_map/all_to_all | solution.py:90
  727.2 46.5 %scatter_custom_fusion.1 = f32[8192,128]{1,0:T(8,128)} fusion(s32[8192]{0:T(1024)S(1)} %bitcast.75, f32[8192,128]{1,0:T(8,128)} %bitcast.8, f32[]{:T(128)} %constant.101.clone.1), kind=kCustom, calls=%fused_computation.62 | custom fusion | flops 1048576 | bytes 4194816 | tf_op jit(solution)/shard_map/scatter-add | solution.py:93
  773.7 5.7 copy.56
  779.4 4.6 bitcast_multiply_fusion
  (889 shorter events, 292.9 us)
Async XLA Ops:
  1.1 9.9 %copy-start = (s32[4096]{0:T(1024)S(1)}, s32[4096]{0:T(1024)}, u32[]{:S(2)}) copy-start(s32[4096]{0:T(1024)} %param.15) | copy-start | bytes 49156
  1.1 9.9 %copy-start.3 = (s32[1,128,64]{1,2,0:T(8,128)S(1)}, s32[1,128,64]{1,2,0:T(8,128)}, u32[]{:S(2)}) copy-start(s32[1,128,64]{1,2,0:T(8,128)} %param.16) | copy-start | bytes 98308
  1.1 91.1 %collective-permute-start = (bf16[1,8,257,128]{3,1,2,0:T(8,128)(2,1)S(1)}, bf16[1,8,257,128]{3,1,2,0:T(8,128)(2,1)S(1)}, u32[]{:S(2)}, u32[]{:S(2)}) collective-permute-start(bf16[1,8,257,128]{3,1,2,0:T(8,128)(2,1)S(1)} %slice.93), channel_id=1, source_target_pairs={{8,0},{16,8},{24,16},{32,24},{40,32},{48,40},{56,48},{64,56},{72,6... | collective-permute-start | bytes 1579016 | tf_op jit(solution)/shard_map/ppermute | solution.py:12
  28.4 17.2 %copy-start.2 = (bf16[162,108]{1,0:T(8,128)(2,1)S(1)}, bf16[162,108]{1,0:T(8,128)(2,1)}, u32[]{:S(2)}) copy-start(bf16[162,108]{1,0:T(8,128)(2,1)} %param.12) | copy-start | bytes 104980
  92.0 9.2 %copy-start.15 = (s32[1,128]{1,0:T(1,128)S(1)}, s32[1,128]{1,0:T(1,128)}, u32[]{:S(2)}) copy-start(s32[1,128]{1,0:T(1,128)} %param.17) | copy-start | bytes 1540
  94.4 18.1 %collective-permute-start.1 = (bf16[17,1,257,128]{3,2,1,0:T(8,128)(2,1)S(1)}, bf16[17,1,257,128]{3,2,1,0:T(8,128)(2,1)S(1)}, u32[]{:S(2)}, u32[]{:S(2)}) collective-permute-start(bf16[17,1,257,128]{3,2,1,0:T(8,128)(2,1)S(1)} %slice.144), channel_id=1, source_target_pairs={{1,0},{2,1},{3,2},{4,3},{5,4},{6,5},{7,6},{9,8},{10,9},{11,10},{12... | collective-permute-start | bytes 3355400 | tf_op jit(solution)/shard_map/ppermute | solution.py:12
  172.1 4.9 copy-start.8
  172.1 4.9 copy-start.9
  172.1 4.9 copy-start.10
  172.1 4.9 copy-start.11
  172.1 4.9 copy-start.12
  172.1 4.9 copy-start.13
  172.1 4.9 copy-start.14
  234.7 4.9 copy-start.8
  234.7 4.9 copy-start.9
  234.7 4.9 copy-start.10
  234.7 4.9 copy-start.11
  234.7 4.9 copy-start.12
  234.7 4.9 copy-start.13
  234.7 4.9 copy-start.14
  297.3 4.9 copy-start.8
  297.3 4.9 copy-start.9
  297.3 4.9 copy-start.10
  297.3 4.9 copy-start.11
  297.3 4.9 copy-start.12
  297.3 4.9 copy-start.13
  297.4 4.9 copy-start.14
  359.9 4.9 copy-start.8
  359.9 4.9 copy-start.9
  359.9 4.9 copy-start.10
  359.9 4.9 copy-start.11
  359.9 4.9 copy-start.12
  359.9 4.9 copy-start.13
  360.0 4.9 copy-start.14
  422.5 4.9 copy-start.8
  422.5 4.9 copy-start.9
  422.5 4.9 copy-start.10
  422.5 4.9 copy-start.11
  422.5 4.9 copy-start.12
  422.5 4.9 copy-start.13
  422.6 4.9 copy-start.14
  485.1 4.9 copy-start.8
  485.1 4.9 copy-start.9
  485.1 4.9 copy-start.10
  485.1 4.9 copy-start.11
  485.1 4.9 copy-start.12
  485.1 4.9 copy-start.13
  485.2 4.9 copy-start.14
  547.7 4.9 copy-start.9
  547.7 4.9 copy-start.10
  547.7 4.9 copy-start.11
  547.7 4.9 copy-start.12
  547.7 4.9 copy-start.13
  547.8 4.9 copy-start.14
  610.3 4.9 copy-start.9
  610.3 4.9 copy-start.10
  610.3 4.9 copy-start.11
  610.3 4.9 copy-start.12
  610.4 4.9 copy-start.13
  610.4 4.9 copy-start.14
  623.2 6.5 copy-start.1
  662.9 11.5 %copy-start.4 = (s32[1,128,64]{1,2,0:T(8,128)S(1)}, s32[1,128,64]{1,2,0:T(8,128)}, u32[]{:S(2)}) copy-start(s32[1,128,64]{1,2,0:T(8,128)} %param.18) | copy-start | bytes 98308
  662.9 11.7 %copy-start.5 = (f32[8192]{0:T(1024)S(1)}, f32[8192]{0:T(1024)}, u32[]{:S(2)}) copy-start(f32[8192]{0:T(1024)} %param.14) | copy-start | bytes 98308
  662.9 64.3 %all-to-all-start = ((f32[128,64,128]{2,1,0:T(8,128)}), f32[128,64,128]{2,1,0:T(8,128)}, u32[]{:S(2)}, u32[]{:S(2)}) async-start(f32[128,64,128]{2,1,0:T(8,128)} %broadcast_select_fusion), calls=%async_computation | async-start | bytes 8388608 | tf_op jit(solution)/shard_map/all_to_all | solution.py:90
  (18 other events, 87.6 us)
where the time goes:
time: 788 us; the launch traced here: 784 us
  local copies, waits for them, and re-layouts  540 us (69%)
  other arithmetic  108 us (14%)
  waiting for transfers between devices  63.2 us (8%)
  matrix products  42.9 us (5%)
  starting transfers between devices  16.1 us (2%)
  loops' own time  13.7 us (2%)
    while x568, local copies, waits for them, and re-layouts  177 us
    gather x3, local copies, waits for them, and re-layouts, on_device(): outgoing = partial_rows[elem_order[send_elem[0]]]  73.6 us
    slice x216, local copies, waits for them, and re-layouts, one_row(): planes[first, second:second + 2 * y_elems - 1:2, third:third + 2 * z_elem...  53.1 us
    all_to_all x1, waiting for transfers between devices, on_device(): lax.all_to_all(outgoing, ('slab', 'cross'), split_axis=0, concat_axis=0,...  52.5 us
    dynamic_update_slice x16, local copies, waits for them, and re-layouts, structured_partials(): per_row = lax.map(one_row, jnp.arange(x_elems, dtype=jnp.int32))  52.5 us
    scatter-add x1, other arithmetic, on_device(): jnp.zeros((param.shape[0], lanes), jnp.float32).at[cell_ids].add(flowing)  46.5 us
    reshape x8, local copies, waits for them, and re-layouts, one_row(): jnp.stack(corner_list, axis=0).reshape(27, row_elems, 2, 4, channels // 8)  44.8 us
    mul x8, local copies, waits for them, and re-layouts, one_row(): product = strain[0] * strain[1]  43.6 us
  transfers between devices with their start and end apart: 3, of which 2 were waited for; matrix products, arithmetic and copies ran while one was open for 12% of the time, Pallas kernels for 0%

commit v1 on v0

v1 whole, which is shorter than its diff:
```python
import functools

import jax
import jax.numpy as jnp
import numpy as np
from jax import lax
from jax.experimental import pallas as pl
from jax.experimental.pallas import tpu as pltpu
from jax.sharding import PartitionSpec as P

AXES = ("slab", "cross")
F32, BF16, I32 = jnp.float32, jnp.bfloat16, jnp.int32
VMEM_BYTES = 56 * 1024 * 1024
ROWS_Q = 168
ROWS_K = 48


def shifted(value, axis):
    count = lax.axis_size(axis)
    return lax.ppermute(value, axis, [(source, source - 1) for source in range(1, count)])


def shifted_both(value):
    slabs, crosses = lax.axis_size("slab"), lax.axis_size("cross")
    pairs = [
        (u * crosses + v, (u - 1) * crosses + v - 1)
        for u in range(1, slabs)
        for v in range(1, crosses)
    ]
    return lax.ppermute(value, AXES, pairs)


def gauss_basis():
    spread = np.sqrt(0.15)
    places = np.array([0.5 - spread, 0.5, 0.5 + spread], np.float32)
    one = np.stack([np.float32(1.0) - places, places], 1).astype(np.float64)
    return np.einsum("ai,bj,ck->abcijk", one, one, one).reshape(27, 8)


def tables():
    q_rows = np.zeros((ROWS_Q, 162), np.float32)
    for m in range(6):
        for g in range(24):
            q_rows[m * 24 + g, 6 * g + m] = 1
        for g in range(3):
            q_rows[144 + (m // 2) * 8 + (m % 2) * 3 + g, 6 * (24 + g) + m] = 1
    cols = np.zeros((108, 3 * ROWS_K), np.float32)
    places = [(0, 0), (0, 1), (1, 0), (1, 1), (2, 0), (2, 1), (0, 2), (1, 2), (2, 2)]
    for i in range(3):
        for place, (j, k) in enumerate(places):
            for c in range(4):
                cols[4 * (9 * i + 3 * j + k) + c, ROWS_K * i + 4 * place + c] = 1
    perm = np.zeros((256, 256), np.float32)
    for f in range(2):
        for d in range(16):
            for s in range(2):
                for c in range(4):
                    perm[(f * 16 + d) * 8 + s * 4 + c, s * 128 + f * 64 + c * 16 + d] = 1
    basis = gauss_basis()
    rows = np.concatenate([basis[:27], basis[24:27], np.zeros((2, 8))], 0).T
    high = rows.astype(np.float32).astype(jnp.bfloat16)
    low = (rows - high.astype(np.float64)).astype(np.float32).astype(jnp.bfloat16)
    eye = np.eye(16)
    block = lambda x: np.einsum("ab,tg->agbt", eye, x.astype(np.float64)).reshape(512, 128)
    split = np.concatenate([block(high), block(low)], 1)
    bf = lambda x: x.astype(jnp.bfloat16)
    return bf(q_rows), bf(cols), bf(perm), bf(split)


def dot(a, b, dims=((1,), (0,))):
    return lax.dot_general(a, b, (dims, ((), ())), preferred_element_type=F32)


def prepare_kernel(order_s, weight, order_v, send, count, placed, slots, turned, spread):
    blocks = weight.shape[1] // 128

    def turn(blk, _):
        at = pl.ds(pl.multiple_of(blk * 128, 128), 128)
        w = weight[:, at]
        rows = jnp.concatenate([w, w[24:27], jnp.zeros((2, 128), F32)], 0)
        turned[at, :] = rows.T
        return 0

    lax.fori_loop(0, blocks, turn, 0)

    def place(step, _):
        for r in range(16):
            e = step * 16 + r
            spread[pl.ds(order_s[e], 1), :] = turned[pl.ds(e, 1), :]
        return 0

    lax.fori_loop(0, blocks * 8, place, 0)

    def back(blk, _):
        at = pl.ds(pl.multiple_of(blk * 128, 128), 128)
        placed[blk] = spread[at, :].T
        return 0

    lax.fori_loop(0, blocks, back, 0)
    live = lax.broadcasted_iota(I32, send.shape, 0) < count[...]
    for part in range(send.shape[0] // 8):
        at = slice(part * 8, part * 8 + 8)
        asked = send[at, :]
        low, high = asked & 127, asked >> 7
        found = jnp.zeros(asked.shape, I32)
        for row in range(blocks):
            table = jnp.broadcast_to(order_v[row : row + 1, :], asked.shape)
            found = jnp.where(high == row, jnp.take_along_axis(table, low, axis=1), found)
        slots[at, :] = jnp.where(live[at, :], found, weight.shape[1])


def partial_kernel(
    slots, odd, even, side_odd, side_even, face, corner, weight, smap, qrow, kcol, perm, basis,
    words, flat, flat_side, taps, mapped, top_part, low_part, rows, low_code, high_code,
):
    step = pl.program_id(0)
    last = pl.num_programs(0) - 1
    elem_rows = 4

    @pl.when(step == 0)
    def _():
        wide = dot(qrow[...], smap[...]).astype(BF16)
        mapped[...] = dot(wide, kcol[...]).astype(BF16)

    def fill(where, plane, side):
        flat[where, 0 : 257 * 8, :] = plane.astype(F32).reshape(257 * 8, 128)
        flat_side[where, 0:257, :] = side.astype(F32)

    def turn(where, slot):
        def line(y, k):
            if y < 8:
                return flat[where, pl.ds(8 * k + y, 128, stride=16), :].astype(BF16)
            return flat_side[where, pl.ds(k, 128, stride=2), :].astype(BF16)

        def ordered(one, other):
            pair = jnp.concatenate([jnp.concatenate(one, 1), jnp.concatenate(other, 1)], 0)
            both = dot(perm[...], pair, ((1,), (1,)))
            return both[:, :128].reshape(32, 8, 128), both[:, 128:].reshape(32, 8, 128)

        def near(y):
            return line(y, 0), line(y, 1)

        def far(y):
            return line(y, 2), line(min(y + 1, 8), 2)

        before, beyond = ordered(near(0), far(0))
        for b in range(elem_rows):
            y = 2 * b
            held = beyond
            middle, after = ordered(near(y + 1), near(y + 2))
            if b % 2 == 0:
                beyond, later = ordered(far(y + 2), far(y + 4))
            else:
                beyond = later
            at = b * ROWS_K
            taps[slot, :, at : at + 16, :] = jnp.concatenate([before, middle], 1).astype(BF16)
            taps[slot, :, at + 16 : at + 32, :] = jnp.concatenate([after, held], 1).astype(BF16)
            taps[slot, :, at + 32 : at + 48, :] = jnp.concatenate([beyond, beyond], 1).astype(BF16)
            before = after

    @pl.when(step > 0)
    def _():
        fill(0, odd[0], side_odd[0])
        turn(0, lax.rem(2 * step + 2, 3))

    @pl.when(step < last)
    def _():
        fill(1, even[0], side_even[0])

    @pl.when(step == last)
    def _():
        fill(1, face[...], corner[...])

    turn(1, lax.rem(2 * step, 3))

    @pl.when(step > 0)
    def _():
        a = step - 1
        plane_slots = [lax.rem(2 * a + i, 3) for i in range(3)]

        def element_row(b, _):
            at = pl.ds(pl.multiple_of(b * ROWS_K, 16), ROWS_K)
            scale = weight[a * elem_rows + b]
            pieces = []
            for d in range(16):
                parts = [
                    jnp.concatenate([taps[s, d, at, :], taps[s, 16 + d, at, :]], 1)
                    for s in plane_slots
                ]
                strain = dot(mapped[...], jnp.concatenate(parts, 0))
                product = strain[:, :128] * strain[:, 128:]
                main = product[0:24]
                for m in range(1, 6):
                    main = main + product[24 * m : 24 * m + 24]
                rest = product[144:152] + product[152:160] + product[160:168]
                summed = jnp.concatenate([main, rest], 0) * scale
                pieces.append(summed)
                if d % 4 == 3:
                    by_elem = jnp.concatenate(pieces, 0).T
                    pieces = []
                    high = by_elem.astype(BF16)
                    to = pl.ds(pl.multiple_of(b * 128, 128), 128)
                    top_part[to, (d - 3) * 32 : (d + 1) * 32] = high
                    low_part[to, (d - 3) * 32 : (d + 1) * 32] = (by_elem - high.astype(F32)).astype(BF16)
            return 0

        lax.fori_loop(0, elem_rows, element_row, 0, unroll=2)
        out_at = pl.ds(pl.multiple_of(a * elem_rows * 128, 128), elem_rows * 128)
        both = dot(top_part[...], basis[...])
        rows[out_at, :] = both[:, :128] + (both[:, 128:] + dot(low_part[...], basis[:, :128]))

    @pl.when(step == last)
    def _():
        count = rows.shape[0]
        chunk = 128

        def largest(i, top):
            block = rows[pl.ds(pl.multiple_of(i * chunk, chunk), chunk), :]
            return jnp.maximum(top, jnp.max(jnp.abs(block).reshape(chunk // 8, 8, 128), 0))

        top = lax.fori_loop(0, count // chunk, largest, jnp.full((8, 128), 1e-30, F32))
        top = jnp.max(jnp.max(top, axis=1, keepdims=True), axis=0, keepdims=True)
        level = jnp.ceil(jnp.log2(jnp.broadcast_to(top, (1, 128))) * 4096.0 + 1.0)
        inverse = jnp.exp2(level * (-1.0 / 4096.0))

        def encode(i, _):
            at = pl.ds(pl.multiple_of(i * chunk, chunk), chunk)
            block = rows[at, :]
            size = jnp.maximum(jnp.abs(block) * inverse, 1e-36)
            root = jnp.exp2(jnp.log2(size) * (1.0 / 3.0)) * 32767.0
            code = jnp.minimum(root + 0.5, 32767.0).astype(I32)
            code = jnp.where(block < 0.0, -code, code)
            low_code[at, :] = code & 65535
            high_code[at, :] = code << 16
            return 0

        lax.fori_loop(0, count // chunk, encode, 0)
        low_code[count : count + 8, :] = jnp.zeros((8, 128), I32)
        high_code[count : count + 8, :] = jnp.zeros((8, 128), I32)

        def gather(o, _):
            for j in range(32):
                first = low_code[pl.ds(slots[j, o], 1), :]
                second = high_code[pl.ds(slots[32 + j, o], 1), :]
                words[o, j] = first | second
            words[o, 32] = level.astype(I32)
            return 0

        lax.fori_loop(0, words.shape[0], gather, 0)


def collect_kernel(cells, words, param, out, *sums):
    count = out.shape[1]

    def clear(i, _):
        for total in sums:
            total[pl.ds(pl.multiple_of(i * 128, 128), 128), :] = jnp.zeros((128, 128), F32)
        return 0

    lax.fori_loop(0, count // 128, clear, 0)

    def add(p, _):
        scale = jnp.exp2(words[p, 32].astype(F32) * (1.0 / 4096.0)) * (1.0 / 32767.0**3)
        for j in range(0, 32, 2):
            ats, values = [], []
            for step in (j, j + 1):
                word = words[p, step]
                for half, where in ((lax.shift_right_arithmetic(word << 16, 16), step),
                                    (lax.shift_right_arithmetic(word, 16), step + 32)):
                    code = half.astype(F32)
                    values.append(code * code * (code * scale))
                    ats.append(pl.ds(cells[where, p], 1))
            held = [total[at, :] for total, at in zip(sums, ats)]
            for total, at, was, value in zip(sums, ats, held, values):
                total[at, :] = was + value
        return 0

    lax.fori_loop(0, words.shape[0], add, 0)

    def finish(i, _):
        at = pl.ds(pl.multiple_of(i * 128, 128), 128)
        total = (sums[0][at, :] + sums[1][at, :]) + (sums[2][at, :] + sums[3][at, :])
        out[:, at] = total.T * jnp.exp(param[pl.ds(i, 1), :])
        return 0

    lax.fori_loop(0, count // 128, finish, 0, unroll=4)


def whole(shape):
    zeros = (0,) * len(shape)
    return pl.BlockSpec(shape, lambda *_: zeros)


def on_device(fields, strain_map, quad_weight, param, elem_order, send_elem, send_count, recv_cell):
    planes = jnp.transpose(fields, (0, 2, 1, 3))
    face = jnp.transpose(shifted(fields[0:1], "slab"), (0, 2, 1, 3))[0]
    side = shifted(fields[:, 0:1], "cross")[:, 0]
    corner = shifted_both(fields[0:1, 0:1])[0, 0]
    q_rows, k_cols, perm, basis = tables()
    elems = elem_order.shape[0]
    smem = pl.BlockSpec(memory_space=pltpu.SMEM)
    vmem = pl.BlockSpec(memory_space=pltpu.VMEM)
    params = pltpu.CompilerParams(vmem_limit_bytes=VMEM_BYTES)

    placed, slots = pl.pallas_call(
        prepare_kernel,
        out_shape=(
            jax.ShapeDtypeStruct((elems // 128, 32, 128), F32),
            jax.ShapeDtypeStruct((64, 128), I32),
        ),
        in_specs=[smem] + [vmem] * 4,
        out_specs=(vmem, vmem),
        scratch_shapes=[pltpu.VMEM((elems, 32), F32), pltpu.VMEM((elems, 32), F32)],
        compiler_params=params,
    )(elem_order, quad_weight, elem_order.reshape(elems // 128, 128), send_elem[0].T, send_count)

    block = (1, 257, 8, 128)
    side_block = (1, 257, 128)
    odd = lambda s: jnp.maximum(2 * s - 1, 1)
    even = lambda s: jnp.minimum(2 * s, 14)
    words = pl.pallas_call(
        partial_kernel,
        grid=(9,),
        out_shape=jax.ShapeDtypeStruct((128, 33, 1, 128), I32),
        in_specs=[
            smem,
            pl.BlockSpec(block, lambda s: (odd(s), 0, 0, 0)),
            pl.BlockSpec(block, lambda s: (even(s), 0, 0, 0)),
            pl.BlockSpec(side_block, lambda s: (odd(s), 0, 0)),
            pl.BlockSpec(side_block, lambda s: (even(s), 0, 0)),
            whole((257, 8, 128)),
            whole((257, 128)),
            whole(placed.shape),
            whole(strain_map.shape),
            whole(q_rows.shape),
            whole(k_cols.shape),
            whole(perm.shape),
            whole(basis.shape),
        ],
        out_specs=whole((128, 33, 1, 128)),
        scratch_shapes=[
            pltpu.VMEM((2, 2080, 128), F32),
            pltpu.VMEM((2, 264, 128), F32),
            pltpu.VMEM((3, 32, 4 * ROWS_K, 128), BF16),
            pltpu.VMEM((ROWS_Q, 3 * ROWS_K), BF16),
            pltpu.VMEM((512, 512), BF16),
            pltpu.VMEM((512, 512), BF16),
            pltpu.VMEM((elems, 128), F32),
            pltpu.VMEM((elems + 8, 128), I32),
            pltpu.VMEM((elems + 8, 128), I32),
        ],
        compiler_params=params,
    )(slots, planes, planes, side, side, face, corner, placed, strain_map, q_rows, k_cols, perm, basis)

    arrived = lax.all_to_all(words, AXES, split_axis=0, concat_axis=0, tiled=True)
    cells = param.shape[0]
    terms = pl.pallas_call(
        collect_kernel,
        out_shape=jax.ShapeDtypeStruct((128, cells), F32),
        in_specs=[smem, vmem, vmem],
        out_specs=vmem,
        scratch_shapes=[pltpu.VMEM((cells, 128), F32)] * 4,
        compiler_params=params,
    )(recv_cell[0].T, arrived, param.reshape(cells // 128, 128))
    return terms.reshape(16, 8, cells)


def solution(mesh):
    return jax.shard_map(
        on_device,
        mesh=mesh,
        in_specs=(
            P("slab", "cross", None, None),
            P(),
            P(None, AXES),
            P(AXES),
            P(AXES),
            P(AXES, None, None),
            P(AXES, None),
            P(AXES, None, None),
        ),
        out_specs=P(None, None, AXES),
        check_vma=False,
    )
```

time: 788 us -> 138 us (0.18)
  local copies, waits for them, and re-layouts: 540 us -> 8.96 us
  other arithmetic: 108 us -> 0 us
  Pallas kernels: 0 us -> 78.4 us
  waiting for transfers between devices: 63.2 us -> 1.07 us
  blocking collectives: 0 us -> 43 us
  matrix products: 42.9 us -> 0 us
  loops' own time: 13.7 us -> 0 us
  starting transfers between devices: 16.1 us -> 5.91 us
    while x568 -> x0, local copies, waits for them, and re-layouts: 177 us -> none
    gather x4 -> x0, local copies, waits for them, and re-layouts: 87.8 us -> none  [the longest x3 73.6 us: on_device(): outgoing = partial_rows[elem_order[send_elem[0]]]]
    pallas_call x0 -> x3, Pallas kernels: none -> 78.4 us  [the longest x1 47.3 us: on_device(): pl.pallas_call(partial_kernel, grid=(9,), out_shape=jax.ShapeDtypeStruct(...]
    all_to_all x1 -> x0, waiting for transfers between devices: 52.5 us -> none  [on_device(): lax.all_to_all(outgoing, ('slab', 'cross'), split_axis=0, concat_axis=0,...]
    dynamic_update_slice x16 -> x0, local copies, waits for them, and re-layouts: 52.5 us -> none  [structured_partials(): per_row = lax.map(one_row, jnp.arange(x_elems, dtype=jnp.int32))]
    slice x218 -> x3, local copies, waits for them, and re-layouts: 55.5 us -> 6.67 us  [the longest x1 4.48 us: on_device(): side = shifted(fields[:, 0:1], 'cross')[:, 0]]
    reshape x10 -> x0, local copies, waits for them, and re-layouts: 46.8 us -> none  [the longest x8 44.8 us: one_row(): jnp.stack(corner_list, axis=0).reshape(27, row_elems, 2, 4, channels // 8)]
    scatter-add x1 -> x0, other arithmetic: 46.5 us -> none  [on_device(): jnp.zeros((param.shape[0], lanes), jnp.float32).at[cell_ids].add(flowing)]
  transfers between devices with their start and end apart: 3 -> 3, of which waited for: 2 -> 1; matrix products, arithmetic and copies ran while one was open for 12% -> 3% of each run, Pallas kernels for 0% -> 9%
where the time goes in v1:
time: 138 us; the launch traced here: 137 us
  Pallas kernels  78.4 us (57%)
  blocking collectives  43 us (31%)
  local copies, waits for them, and re-layouts  8.96 us (6%)
  starting transfers between devices  5.91 us (4%)
    pallas_call x1, Pallas kernels, on_device(): pl.pallas_call(partial_kernel, grid=(9,), out_shape=jax.ShapeDtypeStruct(...  47.3 us
    all_to_all x1, blocking collectives, on_device(): lax.all_to_all(words, AXES, split_axis=0, concat_axis=0, tiled=True)  43 us
    pallas_call x1, Pallas kernels, on_device(): pl.pallas_call(collect_kernel, out_shape=jax.ShapeDtypeStruct((128, cells...  19 us
    pallas_call x1, Pallas kernels, on_device(): pl.pallas_call(prepare_kernel, out_shape=(jax.ShapeDtypeStruct((elems //...  12.1 us
    ppermute x2, starting transfers between devices, shifted(): lax.ppermute(value, axis, [(source, source - 1) for source in range(1, co...  4.62 us
    slice x1, local copies, waits for them, and re-layouts, on_device(): side = shifted(fields[:, 0:1], 'cross')[:, 0]  4.48 us
  transfers between devices with their start and end apart: 3, of which 1 were waited for; matrix products, arithmetic and copies ran while one was open for 3% of the time, Pallas kernels for 9%

profile of v1, /device:TPU:1, one launch (start us, length us, event | category | flops | bytes accessed | tf_op | source)
XLA Modules:
  0.0 137.4 jit_solution(1688805071553791256)
XLA Ops:
  0.0 4.5 %slice.9 = bf16[16,1,257,128]{3,1,2,0:T(2,128)(2,1)S(1)} slice(bf16[16,8,257,128]{3,1,2,0:T(8,128)(2,1)} %param.12), slice={[0:16], [0:1], [0:257], [0:128]} | slice | bytes 2105344 | tf_op jit(solution)/shard_map/slice | solution.py:297
  4.5 0.2 copy.18
  4.7 3.3 %collective-permute-start = (bf16[16,1,257,128]{3,0,2,1:T(8,128)(2,1)S(1)}, bf16[16,1,257,128]{3,0,2,1:T(8,128)(2,1)S(1)}, u32[]{:S(2)}, u32[]{:S(2)}) collective-permute-start(bf16[16,1,257,128]{3,0,2,1:T(8,128)(2,1)S(1)} %copy.18), channel_id=1, source_target_pairs={{1,0},{2,1},{3,2},{4,3},{5,4},{6,5},{7,6},{9,8},{10,9},{11,10},{12... | collective-permute-start | bytes 3158024 | tf_op jit(solution)/shard_map/ppermute | solution.py:20
  8.0 1.1 slice.10
  9.1 1.3 collective-permute-start.1
  10.4 1.1 slice.11
  11.5 1.3 collective-permute-start.2
  12.8 12.1 %shard_map.118 = (f32[32,32,128]{2,1,0:T(8,128)}, s32[64,128]{1,0:T(8,128)}) custom-call(s32[4096]{0:T(1024)} %order_s.1, f32[27,4096]{1,0:T(8,128)} %weight.1, s32[32,128]{1,0:T(8,128)} %bitcast.23, s32[64,128]{1,0:T(8,128)} %bitcast.26, s32[1,128]{1,0:T(1,128)} %count.1), custom_call_target="tpu_custom_call" | custom-call | tf_op jit(solution)/shard_map/pallas_call | solution.py:305
  24.9 0.0 collective-permute-done
  24.9 1.3 copy.21
  26.2 1.1 collective-permute-done.2
  27.2 0.0 copy-start.1
  27.2 0.0 collective-permute-done.1
  27.2 0.0 copy-start
  27.2 0.6 copy-done.1
  27.9 0.2 copy-done
  28.1 47.3 %shard_map.119 = s32[128,33,1,128]{3,2,1,0:T(1,128)} custom-call(s32[64,128]{1,0:T(8,128)} %get-tuple-element.7.slots, bf16[16,257,8,128]{3,2,1,0:T(8,128)(2,1)} %bitcast.17, bf16[16,257,8,128]{3,2,1,0:T(8,128)(2,1)} %bitcast.18, bf16[16,257,128]{2,1,0:T(8,128)(2,1)} %bitcast.19, bf16[16,257,128]{2,1,0:T(8,128)(2,1)} %bitcast.20, ...), custom_call_target="tpu_custom_call" | custom-call | tf_op jit(solution)/shard_map/pallas_call | solution.py:321
  75.4 43.0 %all_to_all.5.words = s32[128,33,1,128]{3,2,1,0:T(1,128)} all-to-all(s32[128,33,1,128]{3,2,1,0:T(1,128)} %shard_map.119), channel_id=1, replica_groups=mesh['slab'=16,'cross'=8] {'slab','cross'}, dimensions={0} | all-to-all | bytes 4325376 | tf_op jit(solution)/shard_map/all_to_all | solution.py:355
  118.4 19.0 %shard_map.120 = f32[128,8192]{1,0:T(8,128)} custom-call(s32[64,128]{1,0:T(8,128)} %bitcast.24, s32[128,33,1,128]{3,2,1,0:T(1,128)} %all_to_all.5.words, f32[64,128]{1,0:T(8,128)} %bitcast.25), custom_call_target="tpu_custom_call" | custom-call | tf_op jit(solution)/shard_map/pallas_call | solution.py:357
  (1 shorter events, 0.0 us)
Async XLA Ops:
  4.7 20.2 %collective-permute-start = (bf16[16,1,257,128]{3,0,2,1:T(8,128)(2,1)S(1)}, bf16[16,1,257,128]{3,0,2,1:T(8,128)(2,1)S(1)}, u32[]{:S(2)}, u32[]{:S(2)}) collective-permute-start(bf16[16,1,257,128]{3,0,2,1:T(8,128)(2,1)S(1)} %copy.18), channel_id=1, source_target_pairs={{1,0},{2,1},{3,2},{4,3},{5,4},{6,5},{7,6},{9,8},{10,9},{11,10},{12... | collective-permute-start | bytes 3158024 | tf_op jit(solution)/shard_map/ppermute | solution.py:20
  9.1 18.1 %collective-permute-start.1 = (bf16[1,8,257,128]{3,1,2,0:T(8,128)(2,1)S(1)}, bf16[1,8,257,128]{3,1,2,0:T(8,128)(2,1)S(1)}, u32[]{:S(2)}, u32[]{:S(2)}) collective-permute-start(bf16[1,8,257,128]{3,1,2,0:T(8,128)(2,1)S(1)} %slice.10), channel_id=1, source_target_pairs={{8,0},{16,8},{24,16},{32,24},{40,32},{48,40},{56,48},{64,56},{72,6... | collective-permute-start | bytes 1579016 | tf_op jit(solution)/shard_map/ppermute | solution.py:20
  11.5 15.7 %collective-permute-start.2 = (bf16[1,1,257,128]{3,2,1,0:T(8,128)(2,1)S(1)}, bf16[1,1,257,128]{3,2,1,0:T(8,128)(2,1)S(1)}, u32[]{:S(2)}, u32[]{:S(2)}) collective-permute-start(bf16[1,1,257,128]{3,2,1,0:T(8,128)(2,1)S(1)} %copy.19), channel_id=1, source_target_pairs={{9,0},{10,1},{11,2},{12,3},{13,4},{14,5},{15,6},{17,8},{18,9},{19,... | collective-permute-start | bytes 197384 | tf_op jit(solution)/shard_map/ppermute | solution.py:30
  27.2 0.6 copy-start.1
  27.2 0.8 copy-start

commit v2 on v1

--- a/solution.py
+++ b/solution.py
@@ -10,9 +10,12 @@
 
 AXES = ("slab", "cross")
 F32, BF16, I32 = jnp.float32, jnp.bfloat16, jnp.int32
-VMEM_BYTES = 56 * 1024 * 1024
+VMEM_BYTES = 36 * 1024 * 1024
 ROWS_Q = 168
 ROWS_K = 48
+HALF = 32
+PITCH = 9
+ODD_FROM = 1168
 
 
 def shifted(value, axis):
@@ -81,12 +84,12 @@
         turned[at, :] = rows.T
         return 0
 
-    lax.fori_loop(0, blocks, turn, 0)
+    lax.fori_loop(0, blocks, turn, 0, unroll=4)
 
     def place(step, _):
-        for r in range(16):
-            e = step * 16 + r
-            spread[pl.ds(order_s[e], 1), :] = turned[pl.ds(e, 1), :]
+        found = [turned[pl.ds(step * 16 + r, 1), :] for r in range(16)]
+        for r, row in enumerate(found):
+            spread[pl.ds(order_s[step * 16 + r], 1), :] = row
         return 0
 
     lax.fori_loop(0, blocks * 8, place, 0)
@@ -96,7 +99,7 @@
         placed[blk] = spread[at, :].T
         return 0
 
-    lax.fori_loop(0, blocks, back, 0)
+    lax.fori_loop(0, blocks, back, 0, unroll=4)
     live = lax.broadcasted_iota(I32, send.shape, 0) < count[...]
     for part in range(send.shape[0] // 8):
         at = slice(part * 8, part * 8 + 8)
@@ -123,13 +126,16 @@
         mapped[...] = dot(wide, kcol[...]).astype(BF16)
 
     def fill(where, plane, side):
-        flat[where, 0 : 257 * 8, :] = plane.astype(F32).reshape(257 * 8, 128)
+        for z in range(257):
+            at = z % 2 * ODD_FROM + z // 2 * PITCH
+            flat[where, at : at + 8, :] = plane[z].astype(F32)
         flat_side[where, 0:257, :] = side.astype(F32)
 
     def turn(where, slot):
         def line(y, k):
             if y < 8:
-                return flat[where, pl.ds(8 * k + y, 128, stride=16), :].astype(BF16)
+                at = k % 2 * ODD_FROM + k // 2 * PITCH + y
+                return flat[where, pl.ds(at, 128, stride=PITCH), :].astype(BF16)
             return flat_side[where, pl.ds(k, 128, stride=2), :].astype(BF16)
 
         def ordered(one, other):
@@ -160,16 +166,16 @@
 
     @pl.when(step > 0)
     def _():
-        fill(0, odd[0], side_odd[0])
+        fill(0, odd.at[0], side_odd[0])
         turn(0, lax.rem(2 * step + 2, 3))
 
     @pl.when(step < last)
     def _():
-        fill(1, even[0], side_even[0])
+        fill(1, even.at[0], side_even[0])
 
     @pl.when(step == last)
     def _():
-        fill(1, face[...], corner[...])
+        fill(1, face, corner[...])
 
     turn(1, lax.rem(2 * step, 3))
 
@@ -204,7 +210,7 @@
                     low_part[to, (d - 3) * 32 : (d + 1) * 32] = (by_elem - high.astype(F32)).astype(BF16)
             return 0
 
-        lax.fori_loop(0, elem_rows, element_row, 0, unroll=2)
+        lax.fori_loop(0, elem_rows, element_row, 0, unroll=4)
         out_at = pl.ds(pl.multiple_of(a * elem_rows * 128, 128), elem_rows * 128)
         both = dot(top_part[...], basis[...])
         rows[out_at, :] = both[:, :128] + (both[:, 128:] + dot(low_part[...], basis[:, :128]))
@@ -239,17 +245,22 @@
         high_code[count : count + 8, :] = jnp.zeros((8, 128), I32)
 
         def gather(o, _):
-            for j in range(32):
-                first = low_code[pl.ds(slots[j, o], 1), :]
-                second = high_code[pl.ds(slots[32 + j, o], 1), :]
-                words[o, j] = first | second
-            words[o, 32] = level.astype(I32)
+            first_row = o * (HALF + 1)
+
+            for group in range(0, HALF, 16):
+                found = []
+                for j in range(group, group + 16):
+                    first = low_code[pl.ds(slots[2 * j, o], 1), :]
+                    found.append(first | high_code[pl.ds(slots[2 * j + 1, o], 1), :])
+                for r, word in enumerate(found):
+                    words[pl.ds(first_row + group + r, 1), :] = word
+            words[pl.ds(first_row + HALF, 1), :] = level.astype(I32)
             return 0
 
-        lax.fori_loop(0, words.shape[0], gather, 0)
-
-
-def collect_kernel(cells, words, param, out, *sums):
+        lax.fori_loop(0, words.shape[0] // (HALF + 1), gather, 0)
+
+
+def collect_kernel(cells, words, param, out, made, sent, *sums):
     count = out.shape[1]
 
     def clear(i, _):
@@ -259,31 +270,47 @@
 
     lax.fori_loop(0, count // 128, clear, 0)
 
-    def add(p, _):
-        scale = jnp.exp2(words[p, 32].astype(F32) * (1.0 / 4096.0)) * (1.0 / 32767.0**3)
-        for j in range(0, 32, 2):
-            ats, values = [], []
-            for step in (j, j + 1):
-                word = words[p, step]
-                for half, where in ((lax.shift_right_arithmetic(word << 16, 16), step),
-                                    (lax.shift_right_arithmetic(word, 16), step + 32)):
-                    code = half.astype(F32)
+    senders = words.shape[0] // (HALF + 1)
+
+    def scale_of(p):
+        level = words[pl.ds(p * (HALF + 1) + HALF, 1), :].astype(F32)
+        return jnp.exp2(level * (1.0 / 4096.0)) * (1.0 / 32767.0**3)
+
+    def add(p, scale):
+        after = scale_of(jnp.minimum(p + 1, senders - 1))
+        first_row = p * (HALF + 1)
+        for group in range(0, HALF, 8):
+            found = [words[pl.ds(first_row + group + r, 1), :] for r in range(8)]
+            values = []
+            for word in found:
+                for half in (word << 16, word):
+                    code = lax.shift_right_arithmetic(half, 16).astype(F32)
                     values.append(code * code * (code * scale))
-                    ats.append(pl.ds(cells[where, p], 1))
-            held = [total[at, :] for total, at in zip(sums, ats)]
-            for total, at, was, value in zip(sums, ats, held, values):
-                total[at, :] = was + value
-        return 0
-
-    lax.fori_loop(0, words.shape[0], add, 0)
-
-    def finish(i, _):
-        at = pl.ds(pl.multiple_of(i * 128, 128), 128)
-        total = (sums[0][at, :] + sums[1][at, :]) + (sums[2][at, :] + sums[3][at, :])
-        out[:, at] = total.T * jnp.exp(param[pl.ds(i, 1), :])
-        return 0
-
-    lax.fori_loop(0, count // 128, finish, 0, unroll=4)
+            for r in range(0, 16, 4):
+                ats = [pl.ds(cells[2 * group + r + t, p], 1) for t in range(4)]
+                held = [total[at, :] for total, at in zip(sums, ats)]
+                for total, at, was, value in zip(sums, ats, held, values[r : r + 4]):
+                    total[at, :] = was + value
+        return after
+
+    lax.fori_loop(0, senders, add, scale_of(0), unroll=2)
+
+    copies = []
+    width = count // sent.shape[0]
+    for part in range(sent.shape[0]):
+
+        def finish(i, _):
+            at = pl.ds(pl.multiple_of(i * 128, 128), 128)
+            total = (sums[0][at, :] + sums[1][at, :]) + (sums[2][at, :] + sums[3][at, :])
+            made[:, at] = total.T * jnp.exp(param[pl.ds(i, 1), :])
+            return 0
+
+        lax.fori_loop(part * width // 128, (part + 1) * width // 128, finish, 0, unroll=4)
+        at = pl.ds(part * width, width)
+        copies.append(pltpu.make_async_copy(made.at[:, at], out.at[:, at], sent.at[part]))
+        copies[-1].start()
+    for copy in copies:
+        copy.wait()
 
 
 def whole(shape):
@@ -294,8 +321,8 @@
 def on_device(fields, strain_map, quad_weight, param, elem_order, send_elem, send_count, recv_cell):
     planes = jnp.transpose(fields, (0, 2, 1, 3))
     face = jnp.transpose(shifted(fields[0:1], "slab"), (0, 2, 1, 3))[0]
+    corner = shifted_both(fields[0:1, 0:1])[0, 0]
     side = shifted(fields[:, 0:1], "cross")[:, 0]
-    corner = shifted_both(fields[0:1, 0:1])[0, 0]
     q_rows, k_cols, perm, basis = tables()
     elems = elem_order.shape[0]
     smem = pl.BlockSpec(memory_space=pltpu.SMEM)
@@ -321,7 +348,7 @@
     words = pl.pallas_call(
         partial_kernel,
         grid=(9,),
-        out_shape=jax.ShapeDtypeStruct((128, 33, 1, 128), I32),
+        out_shape=jax.ShapeDtypeStruct((128 * 33, 128), I32),
         in_specs=[
             smem,
             pl.BlockSpec(block, lambda s: (odd(s), 0, 0, 0)),
@@ -337,9 +364,9 @@
             whole(perm.shape),
             whole(basis.shape),
         ],
-        out_specs=whole((128, 33, 1, 128)),
+        out_specs=whole((128 * 33, 128)),
         scratch_shapes=[
-            pltpu.VMEM((2, 2080, 128), F32),
+            pltpu.VMEM((2, 2 * ODD_FROM, 128), F32),
             pltpu.VMEM((2, 264, 128), F32),
             pltpu.VMEM((3, 32, 4 * ROWS_K, 128), BF16),
             pltpu.VMEM((ROWS_Q, 3 * ROWS_K), BF16),
@@ -352,16 +379,17 @@
         compiler_params=params,
     )(slots, planes, planes, side, side, face, corner, placed, strain_map, q_rows, k_cols, perm, basis)
 
-    arrived = lax.all_to_all(words, AXES, split_axis=0, concat_axis=0, tiled=True)
+    arrived = lax.all_to_all(words.reshape(128, 33, 1, 128), AXES, split_axis=0, concat_axis=0, tiled=True)
     cells = param.shape[0]
     terms = pl.pallas_call(
         collect_kernel,
         out_shape=jax.ShapeDtypeStruct((128, cells), F32),
         in_specs=[smem, vmem, vmem],
-        out_specs=vmem,
-        scratch_shapes=[pltpu.VMEM((cells, 128), F32)] * 4,
+        out_specs=pl.BlockSpec(memory_space=pl.ANY),
+        scratch_shapes=[pltpu.VMEM((128, cells), F32), pltpu.SemaphoreType.DMA((8,))]
+        + [pltpu.VMEM((cells, 128), F32)] * 4,
         compiler_params=params,
-    )(recv_cell[0].T, arrived, param.reshape(cells // 128, 128))
+    )(recv_cell[0].T, arrived.reshape(128 * 33, 128), param.reshape(cells // 128, 128))
     return terms.reshape(16, 8, cells)
 
 

time: 138 us -> 125 us (0.906)
  Pallas kernels: 78.4 us -> 61.4 us
  waiting for transfers between devices: 1.07 us -> 4.74 us
    pallas_call x1, Pallas kernels: 47.3 us -> 37.4 us  [on_device(): pl.pallas_call(partial_kernel, grid=(9,), out_shape=jax.ShapeDtypeStruct(...]
    pallas_call x1, Pallas kernels: 12.1 us -> 7.52 us  [on_device(): pl.pallas_call(prepare_kernel, out_shape=(jax.ShapeDtypeStruct((elems //...]
    ppermute x1, waiting for transfers between devices: 1.06 us -> 4.74 us  [shifted_both(): return lax.ppermute(value, AXES, pairs)]
    pallas_call x1, Pallas kernels: 19 us -> 16.4 us  [on_device(): pl.pallas_call(collect_kernel, out_shape=jax.ShapeDtypeStruct((128, cells...]
  transfers between devices with their start and end apart: 3 -> 3, of which waited for: 1 -> 1; matrix products, arithmetic and copies ran while one was open for 3% -> 2% of each run, Pallas kernels for 9% -> 6%
where the time goes in v2:
time: 125 us; the launch traced here: 124 us
  Pallas kernels  61.4 us (49%)
  blocking collectives  42.6 us (34%)
  local copies, waits for them, and re-layouts  9.14 us (7%)
  starting transfers between devices  6.05 us (5%)
  waiting for transfers between devices  4.74 us (4%)
    all_to_all x1, blocking collectives, on_device(): lax.all_to_all(words.reshape(128, 33, 1, 128), AXES, split_axis=0, concat...  42.6 us
    pallas_call x1, Pallas kernels, on_device(): pl.pallas_call(partial_kernel, grid=(9,), out_shape=jax.ShapeDtypeStruct(...  37.4 us
    pallas_call x1, Pallas kernels, on_device(): pl.pallas_call(collect_kernel, out_shape=jax.ShapeDtypeStruct((128, cells...  16.4 us
    pallas_call x1, Pallas kernels, on_device(): pl.pallas_call(prepare_kernel, out_shape=(jax.ShapeDtypeStruct((elems //...  7.52 us
    ppermute x2, starting transfers between devices, shifted(): lax.ppermute(value, axis, [(source, source - 1) for source in range(1, co...  4.75 us
    ppermute x1, waiting for transfers between devices, shifted_both(): return lax.ppermute(value, AXES, pairs)  4.74 us
    slice x1, local copies, waits for them, and re-layouts, on_device(): side = shifted(fields[:, 0:1], 'cross')[:, 0]  4.63 us
  transfers between devices with their start and end apart: 3, of which 1 were waited for; matrix products, arithmetic and copies ran while one was open for 2% of the time, Pallas kernels for 6%

profile of v2, /device:TPU:1, one launch (start us, length us, event | category | flops | bytes accessed | tf_op | source)
XLA Modules:
  0.0 124.1 jit_solution(9139239634569965205)
XLA Ops:
  0.0 0.0 copy-start
  0.0 4.6 %slice.9 = bf16[16,1,257,128]{3,1,2,0:T(2,128)(2,1)S(1)} slice(bf16[16,8,257,128]{3,1,2,0:T(8,128)(2,1)} %param.12), slice={[0:16], [0:1], [0:257], [0:128]} | slice | bytes 2105344 | tf_op jit(solution)/shard_map/slice | solution.py:325
  4.6 0.0 copy-start.5
  4.6 0.0 copy-start.11
  4.7 0.2 copy.21
  4.8 0.0 copy-start.2
  4.9 0.0 copy-start.3
  4.9 0.0 copy-start.7
  4.9 3.5 %collective-permute-start = (bf16[16,1,257,128]{3,0,2,1:T(8,128)(2,1)S(1)}, bf16[16,1,257,128]{3,0,2,1:T(8,128)(2,1)S(1)}, u32[]{:S(2)}, u32[]{:S(2)}) collective-permute-start(bf16[16,1,257,128]{3,0,2,1:T(8,128)(2,1)S(1)} %copy.21), channel_id=1, source_target_pairs={{1,0},{2,1},{3,2},{4,3},{5,4},{6,5},{7,6},{9,8},{10,9},{11,10},{12... | collective-permute-start | bytes 3158024 | tf_op jit(solution)/shard_map/ppermute | solution.py:23
  8.4 1.1 slice.10
  9.4 1.3 %collective-permute-start.1 = (bf16[1,8,257,128]{3,1,2,0:T(8,128)(2,1)S(1)}, bf16[1,8,257,128]{3,1,2,0:T(8,128)(2,1)S(1)}, u32[]{:S(2)}, u32[]{:S(2)}) collective-permute-start(bf16[1,8,257,128]{3,1,2,0:T(8,128)(2,1)S(1)} %slice.10), channel_id=1, source_target_pairs={{8,0},{16,8},{24,16},{32,24},{40,32},{48,40},{56,48},{64,56},{72,6... | collective-permute-start | bytes 1579016 | tf_op jit(solution)/shard_map/ppermute | solution.py:23
  10.7 1.1 slice.11
  11.9 1.3 %collective-permute-start.2 = (bf16[1,1,257,128]{3,2,1,0:T(8,128)(2,1)S(1)}, bf16[1,1,257,128]{3,2,1,0:T(8,128)(2,1)S(1)}, u32[]{:S(2)}, u32[]{:S(2)}) collective-permute-start(bf16[1,1,257,128]{3,2,1,0:T(8,128)(2,1)S(1)} %copy.22), channel_id=1, source_target_pairs={{9,0},{10,1},{11,2},{12,3},{13,4},{14,5},{15,6},{17,8},{18,9},{19,... | collective-permute-start | bytes 197384 | tf_op jit(solution)/shard_map/ppermute | solution.py:33
  13.2 0.0 copy-done.5
  13.2 0.0 copy-done.11
  13.2 0.0 copy-start.1
  13.2 1.0 copy-done.1
  14.2 0.0 copy-start.10
  14.2 0.8 copy-done.10
  15.0 0.0 copy-start.4
  15.0 0.0 copy-start.6
  15.0 7.5 %shard_map.118 = (f32[32,32,128]{2,1,0:T(8,128)S(1)}, s32[64,128]{1,0:T(8,128)S(1)}) custom-call(s32[4096]{0:T(1024)S(1)} %copy-done.5, f32[27,4096]{1,0:T(8,128)S(1)} %copy-done.1, s32[32,128]{1,0:T(8,128)S(1)} %bitcast.27, s32[64,128]{1,0:T(8,128)S(1)} %bitcast.30, s32[1,128]{1,0:T(1,128)S(1)} %copy-done.11), custom_call_target="tpu_custom_call" | custom-call | tf_op jit(solution)/shard_map/pallas_call | solution.py:332
  22.5 0.0 collective-permute-done
  22.5 0.3 copy.24
  22.8 4.7 %collective-permute-done.2 = bf16[1,1,257,128]{3,2,1,0:T(8,128)(2,1)S(1)} collective-permute-done((bf16[1,1,257,128]{3,2,1,0:T(8,128)(2,1)S(1)}, bf16[1,1,257,128]{3,2,1,0:T(8,128)(2,1)S(1)}, u32[]{:S(2)}, u32[]{:S(2)}) %collective-permute-start.2) | collective-permute-done | bytes 65824 | tf_op jit(solution)/shard_map/ppermute | solution.py:33
  27.6 0.0 collective-permute-done.1
  27.6 0.0 copy-done
  27.6 0.0 copy-done.2
  27.6 0.0 copy-done.3
  27.6 0.0 copy-done.7
  27.6 0.0 copy-done.4
  27.6 0.0 copy-done.6
  27.6 37.4 %shard_map.119 = s32[4224,128]{1,0:T(8,128)S(1)} custom-call(s32[64,128]{1,0:T(8,128)S(1)} %get-tuple-element.7.slots, bf16[16,257,8,128]{3,2,1,0:T(8,128)(2,1)S(1)} %bitcast.19, bf16[16,257,8,128]{3,2,1,0:T(8,128)(2,1)S(1)} %bitcast.20, bf16[16,257,128]{2,1,0:T(8,128)(2,1)S(1)} %bitcast.21, bf16[16,257,128]{2,1,0:T(8,128)(2,1)S(1)} %bitcast.22, ...), custom_call_target="tpu_custom_call" | custom-call | tf_op jit(solution)/shard_map/pallas_call | solution.py:348
  65.1 0.0 copy-start.8
  65.1 0.0 copy-start.9
  65.1 42.6 %all_to_all.5 = s32[128,33,1,128]{3,2,1,0:T(1,128)S(1)} all-to-all(s32[128,33,1,128]{3,2,1,0:T(1,128)S(1)} %bitcast.23), channel_id=1, replica_groups=mesh['slab'=16,'cross'=8] {'slab','cross'}, dimensions={0} | all-to-all | bytes 4325376 | tf_op jit(solution)/shard_map/all_to_all | solution.py:382
  107.7 0.0 copy-done.8
  107.7 0.0 copy-done.9
  107.7 16.4 %shard_map.120 = f32[128,8192]{1,0:T(8,128)} custom-call(s32[64,128]{1,0:T(8,128)S(1)} %bitcast.28, s32[4224,128]{1,0:T(8,128)S(1)} %bitcast.24, f32[64,128]{1,0:T(8,128)S(1)} %bitcast.29), custom_call_target="tpu_custom_call" | custom-call | tf_op jit(solution)/shard_map/pallas_call | solution.py:384
  (1 shorter events, 0.0 us)
Async XLA Ops:
  0.0 27.6 %copy-start = (bf16[16,8,257,128]{3,1,2,0:T(8,128)(2,1)S(1)}, bf16[16,8,257,128]{3,1,2,0:T(8,128)(2,1)}, u32[]{:S(2)}) copy-start(bf16[16,8,257,128]{3,1,2,0:T(8,128)(2,1)} %param.12) | copy-start | bytes 25264132
  4.6 8.5 %copy-start.5 = (s32[4096]{0:T(1024)S(1)}, s32[4096]{0:T(1024)}, u32[]{:S(2)}) copy-start(s32[4096]{0:T(1024)} %order_s.1) | copy-start | bytes 49156
  4.6 8.5 %copy-start.11 = (s32[1,128]{1,0:T(1,128)S(1)}, s32[1,128]{1,0:T(1,128)}, u32[]{:S(2)}) copy-start(s32[1,128]{1,0:T(1,128)} %count.1) | copy-start | bytes 1540
  4.8 22.7 %copy-start.2 = (bf16[512,256]{1,0:T(8,128)(2,1)S(1)}, bf16[512,256]{1,0:T(8,128)(2,1)}, u32[]{:S(2)}) copy-start(bf16[512,256]{1,0:T(8,128)(2,1)} %constant.11.clone.basis) | copy-start | bytes 786436
  4.9 22.7 %copy-start.3 = (bf16[256,256]{1,0:T(8,128)(2,1)S(1)}, bf16[256,256]{1,0:T(8,128)(2,1)}, u32[]{:S(2)}) copy-start(bf16[256,256]{1,0:T(8,128)(2,1)} %constant.10.clone.perm) | copy-start | bytes 393220
  4.9 22.7 %copy-start.7 = (bf16[162,108]{1,0:T(8,128)(2,1)S(1)}, bf16[162,108]{1,0:T(8,128)(2,1)}, u32[]{:S(2)}) copy-start(bf16[162,108]{1,0:T(8,128)(2,1)} %smap.1) | copy-start | bytes 104980
  4.9 17.7 %collective-permute-start = (bf16[16,1,257,128]{3,0,2,1:T(8,128)(2,1)S(1)}, bf16[16,1,257,128]{3,0,2,1:T(8,128)(2,1)S(1)}, u32[]{:S(2)}, u32[]{:S(2)}) collective-permute-start(bf16[16,1,257,128]{3,0,2,1:T(8,128)(2,1)S(1)} %copy.21), channel_id=1, source_target_pairs={{1,0},{2,1},{3,2},{4,3},{5,4},{6,5},{7,6},{9,8},{10,9},{11,10},{12... | collective-permute-start | bytes 3158024 | tf_op jit(solution)/shard_map/ppermute | solution.py:23
  9.4 18.1 %collective-permute-start.1 = (bf16[1,8,257,128]{3,1,2,0:T(8,128)(2,1)S(1)}, bf16[1,8,257,128]{3,1,2,0:T(8,128)(2,1)S(1)}, u32[]{:S(2)}, u32[]{:S(2)}) collective-permute-start(bf16[1,8,257,128]{3,1,2,0:T(8,128)(2,1)S(1)} %slice.10), channel_id=1, source_target_pairs={{8,0},{16,8},{24,16},{32,24},{40,32},{48,40},{56,48},{64,56},{72,6... | collective-permute-start | bytes 1579016 | tf_op jit(solution)/shard_map/ppermute | solution.py:23
  11.9 15.7 %collective-permute-start.2 = (bf16[1,1,257,128]{3,2,1,0:T(8,128)(2,1)S(1)}, bf16[1,1,257,128]{3,2,1,0:T(8,128)(2,1)S(1)}, u32[]{:S(2)}, u32[]{:S(2)}) collective-permute-start(bf16[1,1,257,128]{3,2,1,0:T(8,128)(2,1)S(1)} %copy.22), channel_id=1, source_target_pairs={{9,0},{10,1},{11,2},{12,3},{13,4},{14,5},{15,6},{17,8},{18,9},{19,... | collective-permute-start | bytes 197384 | tf_op jit(solution)/shard_map/ppermute | solution.py:33
  13.2 1.0 copy-start.1
  14.2 0.8 copy-start.10
  15.0 12.6 %copy-start.4 = (bf16[168,162]{1,0:T(8,128)(2,1)S(1)}, bf16[168,162]{1,0:T(8,128)(2,1)}, u32[]{:S(2)}) copy-start(bf16[168,162]{1,0:T(8,128)(2,1)} %constant.8.clone.qrow) | copy-start | bytes 163300
  15.0 12.6 %copy-start.6 = (bf16[108,144]{1,0:T(8,128)(2,1)S(1)}, bf16[108,144]{1,0:T(8,128)(2,1)}, u32[]{:S(2)}) copy-start(bf16[108,144]{1,0:T(8,128)(2,1)} %constant.9.clone.kcol) | copy-start | bytes 93316
  65.1 42.6 %copy-start.8 = (s32[1,128,64]{1,2,0:T(8,128)S(1)}, s32[1,128,64]{1,2,0:T(8,128)}, u32[]{:S(2)}) copy-start(s32[1,128,64]{1,2,0:T(8,128)} %param.19) | copy-start | bytes 98308
  65.1 42.6 %copy-start.9 = (f32[8192]{0:T(1024)S(1)}, f32[8192]{0:T(1024)}, u32[]{:S(2)}) copy-start(f32[8192]{0:T(1024)} %param.15) | copy-start | bytes 98308

commit v3 on v2

--- a/solution.py
+++ b/solution.py
@@ -74,7 +74,13 @@
     return lax.dot_general(a, b, (dims, ((), ())), preferred_element_type=F32)
 
 
-def prepare_kernel(order_s, weight, order_v, send, count, placed, slots, turned, spread):
+def paired(upper, lower):
+    return upper | (lower << 16)
+
+
+def prepare_kernel(
+    order_s, weight, order_v, send, count, cells, placed, slots, places, turned, spread
+):
     blocks = weight.shape[1] // 128
 
     def turn(blk, _):
@@ -101,6 +107,7 @@
 
     lax.fori_loop(0, blocks, back, 0, unroll=4)
     live = lax.broadcasted_iota(I32, send.shape, 0) < count[...]
+    looked_up = []
     for part in range(send.shape[0] // 8):
         at = slice(part * 8, part * 8 + 8)
         asked = send[at, :]
@@ -109,7 +116,11 @@
         for row in range(blocks):
             table = jnp.broadcast_to(order_v[row : row + 1, :], asked.shape)
             found = jnp.where(high == row, jnp.take_along_axis(table, low, axis=1), found)
-        slots[at, :] = jnp.where(live[at, :], found, weight.shape[1])
+        looked_up.append(jnp.where(live[at, :], found, weight.shape[1]))
+    for part in range(HALF // 8):
+        at = slice(part * 8, part * 8 + 8)
+        slots[at, :] = paired(looked_up[part], looked_up[part + HALF // 8])
+    places[...] = paired(cells[:HALF, :], cells[HALF:, :])
 
 
 def partial_kernel(
@@ -250,8 +261,9 @@
             for group in range(0, HALF, 16):
                 found = []
                 for j in range(group, group + 16):
-                    first = low_code[pl.ds(slots[2 * j, o], 1), :]
-                    found.append(first | high_code[pl.ds(slots[2 * j + 1, o], 1), :])
+                    pair = slots[j, o]
+                    first = low_code[pl.ds(pair & 65535, 1), :]
+                    found.append(first | high_code[pl.ds(lax.shift_right_logical(pair, 16), 1), :])
                 for r, word in enumerate(found):
                     words[pl.ds(first_row + group + r, 1), :] = word
             words[pl.ds(first_row + HALF, 1), :] = level.astype(I32)
@@ -287,7 +299,12 @@
                     code = lax.shift_right_arithmetic(half, 16).astype(F32)
                     values.append(code * code * (code * scale))
             for r in range(0, 16, 4):
-                ats = [pl.ds(cells[2 * group + r + t, p], 1) for t in range(4)]
+                pairs = [cells[group + r // 2 + t, p] for t in range(2)]
+                ats = [
+                    pl.ds(at, 1)
+                    for pair in pairs
+                    for at in (pair & 65535, lax.shift_right_logical(pair, 16))
+                ]
                 held = [total[at, :] for total, at in zip(sums, ats)]
                 for total, at, was, value in zip(sums, ats, held, values[r : r + 4]):
                     total[at, :] = was + value
@@ -329,17 +346,18 @@
     vmem = pl.BlockSpec(memory_space=pltpu.VMEM)
     params = pltpu.CompilerParams(vmem_limit_bytes=VMEM_BYTES)
 
-    placed, slots = pl.pallas_call(
+    placed, slots, places = pl.pallas_call(
         prepare_kernel,
         out_shape=(
             jax.ShapeDtypeStruct((elems // 128, 32, 128), F32),
-            jax.ShapeDtypeStruct((64, 128), I32),
+            jax.ShapeDtypeStruct((HALF, 128), I32),
+            jax.ShapeDtypeStruct((HALF, 128), I32),
         ),
-        in_specs=[smem] + [vmem] * 4,
-        out_specs=(vmem, vmem),
+        in_specs=[smem] + [vmem] * 5,
+        out_specs=(vmem, vmem, vmem),
         scratch_shapes=[pltpu.VMEM((elems, 32), F32), pltpu.VMEM((elems, 32), F32)],
         compiler_params=params,
-    )(elem_order, quad_weight, elem_order.reshape(elems // 128, 128), send_elem[0].T, send_count)
+    )(elem_order, quad_weight, elem_order.reshape(elems // 128, 128), send_elem[0].T, send_count, recv_cell[0].T)
 
     block = (1, 257, 8, 128)
     side_block = (1, 257, 128)
@@ -389,7 +407,7 @@
         scratch_shapes=[pltpu.VMEM((128, cells), F32), pltpu.SemaphoreType.DMA((8,))]
         + [pltpu.VMEM((cells, 128), F32)] * 4,
         compiler_params=params,
-    )(recv_cell[0].T, arrived.reshape(128 * 33, 128), param.reshape(cells // 128, 128))
+    )(places, arrived.reshape(128 * 33, 128), param.reshape(cells // 128, 128))
     return terms.reshape(16, 8, cells)
 
 

time: 125 us -> 123 us (0.984)
  Pallas kernels: 61.4 us -> 59.8 us
    pallas_call x1, Pallas kernels: 37.4 us -> 36.2 us  [on_device(): pl.pallas_call(partial_kernel, grid=(9,), out_shape=jax.ShapeDtypeStruct(...]
where the time goes in v3:
time: 123 us
  Pallas kernels  59.8 us (49%)
  blocking collectives  42.6 us (35%)
  local copies, waits for them, and re-layouts  9.89 us (8%)
  starting transfers between devices  6.05 us (5%)
  waiting for transfers between devices  3.98 us (3%)
    all_to_all x1, blocking collectives, on_device(): lax.all_to_all(words.reshape(128, 33, 1, 128), AXES, split_axis=0, concat...  42.6 us
    pallas_call x1, Pallas kernels, on_device(): pl.pallas_call(partial_kernel, grid=(9,), out_shape=jax.ShapeDtypeStruct(...  36.2 us
    pallas_call x1, Pallas kernels, on_device(): pl.pallas_call(collect_kernel, out_shape=jax.ShapeDtypeStruct((128, cells...  16.1 us
    pallas_call x1, Pallas kernels, on_device(): pl.pallas_call(prepare_kernel, out_shape=(jax.ShapeDtypeStruct((elems //...  7.53 us
    ppermute x2, starting transfers between devices, shifted(): lax.ppermute(value, axis, [(source, source - 1) for source in range(1, co...  4.75 us
    slice x1, local copies, waits for them, and re-layouts, on_device(): side = shifted(fields[:, 0:1], 'cross')[:, 0]  4.63 us
    ppermute x1, waiting for transfers between devices, shifted_both(): return lax.ppermute(value, AXES, pairs)  3.98 us
    unnamed x26, local copies, waits for them, and re-layouts  2.8 us
  transfers between devices with their start and end apart: 3, of which 1 were waited for; matrix products, arithmetic and copies ran while one was open for 2% of the time, Pallas kernels for 6%

profile of v3, /device:TPU:1, one launch (start us, length us, event | category | flops | bytes accessed | tf_op | source)
XLA Modules:
  0.0 122.5 jit_solution(3731360613826851840)
XLA Ops:
  0.0 0.0 copy-start
  0.0 4.6 %slice.9 = bf16[16,1,257,128]{3,1,2,0:T(2,128)(2,1)S(1)} slice(bf16[16,8,257,128]{3,1,2,0:T(8,128)(2,1)} %param.12), slice={[0:16], [0:1], [0:257], [0:128]} | slice | bytes 2105344 | tf_op jit(solution)/shard_map/slice | solution.py:342
  4.6 0.0 copy-start.5
  4.6 0.0 copy-start.11
  4.7 0.2 copy.21
  4.8 0.0 copy-start.2
  4.9 0.0 copy-start.3
  4.9 0.0 copy-start.6
  4.9 3.5 %collective-permute-start = (bf16[16,1,257,128]{3,0,2,1:T(8,128)(2,1)S(1)}, bf16[16,1,257,128]{3,0,2,1:T(8,128)(2,1)S(1)}, u32[]{:S(2)}, u32[]{:S(2)}) collective-permute-start(bf16[16,1,257,128]{3,0,2,1:T(8,128)(2,1)S(1)} %copy.21), channel_id=1, source_target_pairs={{1,0},{2,1},{3,2},{4,3},{5,4},{6,5},{7,6},{9,8},{10,9},{11,10},{12... | collective-permute-start | bytes 3158024 | tf_op jit(solution)/shard_map/ppermute | solution.py:23
  8.4 1.1 slice.10
  9.4 1.3 %collective-permute-start.1 = (bf16[1,8,257,128]{3,1,2,0:T(8,128)(2,1)S(1)}, bf16[1,8,257,128]{3,1,2,0:T(8,128)(2,1)S(1)}, u32[]{:S(2)}, u32[]{:S(2)}) collective-permute-start(bf16[1,8,257,128]{3,1,2,0:T(8,128)(2,1)S(1)} %slice.10), channel_id=1, source_target_pairs={{8,0},{16,8},{24,16},{32,24},{40,32},{48,40},{56,48},{64,56},{72,6... | collective-permute-start | bytes 1579016 | tf_op jit(solution)/shard_map/ppermute | solution.py:23
  10.7 1.1 slice.11
  11.9 1.3 %collective-permute-start.2 = (bf16[1,1,257,128]{3,2,1,0:T(8,128)(2,1)S(1)}, bf16[1,1,257,128]{3,2,1,0:T(8,128)(2,1)S(1)}, u32[]{:S(2)}, u32[]{:S(2)}) collective-permute-start(bf16[1,1,257,128]{3,2,1,0:T(8,128)(2,1)S(1)} %copy.22), channel_id=1, source_target_pairs={{9,0},{10,1},{11,2},{12,3},{13,4},{14,5},{15,6},{17,8},{18,9},{19,... | collective-permute-start | bytes 197384 | tf_op jit(solution)/shard_map/ppermute | solution.py:33
  13.2 0.0 copy-done.5
  13.2 0.0 copy-done.11
  13.2 0.0 copy-start.1
  13.2 1.0 copy-done.1
  14.2 0.0 copy-start.9
  14.2 0.8 copy-done.9
  15.0 0.0 copy-start.10
  15.0 0.8 copy-done.10
  15.8 0.0 copy-start.4
  15.8 0.0 copy-start.7
  15.8 7.5 %shard_map.118 = (f32[32,32,128]{2,1,0:T(8,128)S(1)}, s32[32,128]{1,0:T(8,128)S(1)}, s32[32,128]{1,0:T(8,128)S(1)}) custom-call(s32[4096]{0:T(1024)S(1)} %copy-done.5, f32[27,4096]{1,0:T(8,128)S(1)} %copy-done.1, s32[32,128]{1,0:T(8,128)S(1)} %bitcast.27, s32[64,128]{1,0:T(8,128)S(1)} %bitcast.29, s32[1,128]{1,0:T(1,128)S(1)} %copy-done.11, ...), custom_call_target="tpu_custom_call" | custom-call | tf_op jit(solution)/shard_map/pallas_call | solution.py:349
  23.3 0.0 collective-permute-done
  23.3 0.3 copy.24
  23.6 4.0 %collective-permute-done.2 = bf16[1,1,257,128]{3,2,1,0:T(8,128)(2,1)S(1)} collective-permute-done((bf16[1,1,257,128]{3,2,1,0:T(8,128)(2,1)S(1)}, bf16[1,1,257,128]{3,2,1,0:T(8,128)(2,1)S(1)}, u32[]{:S(2)}, u32[]{:S(2)}) %collective-permute-start.2) | collective-permute-done | bytes 65824 | tf_op jit(solution)/shard_map/ppermute | solution.py:33
  27.6 0.0 collective-permute-done.1
  27.6 0.0 copy-done
  27.6 0.0 copy-done.2
  27.6 0.0 copy-done.3
  27.6 0.0 copy-done.6
  27.6 0.0 copy-done.4
  27.6 0.0 copy-done.7
  27.6 36.2 %shard_map.119 = s32[4224,128]{1,0:T(8,128)S(1)} custom-call(s32[32,128]{1,0:T(8,128)S(1)} %get-tuple-element.9.slots, bf16[16,257,8,128]{3,2,1,0:T(8,128)(2,1)S(1)} %bitcast.19, bf16[16,257,8,128]{3,2,1,0:T(8,128)(2,1)S(1)} %bitcast.20, bf16[16,257,128]{2,1,0:T(8,128)(2,1)S(1)} %bitcast.21, bf16[16,257,128]{2,1,0:T(8,128)(2,1)S(1)} %bitcast.22, ...), custom_call_target="tpu_custom_call" | custom-call | tf_op jit(solution)/shard_map/pallas_call | solution.py:366
  63.8 0.0 copy-start.8
  63.8 42.6 %all_to_all.5 = s32[128,33,1,128]{3,2,1,0:T(1,128)S(1)} all-to-all(s32[128,33,1,128]{3,2,1,0:T(1,128)S(1)} %bitcast.24), channel_id=1, replica_groups=mesh['slab'=16,'cross'=8] {'slab','cross'}, dimensions={0} | all-to-all | bytes 4325376 | tf_op jit(solution)/shard_map/all_to_all | solution.py:400
  106.4 0.0 copy-done.8
  106.4 16.1 %shard_map.120 = f32[128,8192]{1,0:T(8,128)} custom-call(s32[32,128]{1,0:T(8,128)S(1)} %get-tuple-element.8.cells, s32[4224,128]{1,0:T(8,128)S(1)} %bitcast.23, f32[64,128]{1,0:T(8,128)S(1)} %bitcast.28), custom_call_target="tpu_custom_call" | custom-call | tf_op jit(solution)/shard_map/pallas_call | solution.py:402
  (1 shorter events, 0.0 us)
Async XLA Ops:
  0.0 27.6 %copy-start = (bf16[16,8,257,128]{3,1,2,0:T(8,128)(2,1)S(1)}, bf16[16,8,257,128]{3,1,2,0:T(8,128)(2,1)}, u32[]{:S(2)}) copy-start(bf16[16,8,257,128]{3,1,2,0:T(8,128)(2,1)} %param.12) | copy-start | bytes 25264132
  4.6 8.5 %copy-start.5 = (s32[4096]{0:T(1024)S(1)}, s32[4096]{0:T(1024)}, u32[]{:S(2)}) copy-start(s32[4096]{0:T(1024)} %order_s.1) | copy-start | bytes 49156
  4.6 8.5 %copy-start.11 = (s32[1,128]{1,0:T(1,128)S(1)}, s32[1,128]{1,0:T(1,128)}, u32[]{:S(2)}) copy-start(s32[1,128]{1,0:T(1,128)} %count.1) | copy-start | bytes 1540
  4.8 22.7 %copy-start.2 = (bf16[512,256]{1,0:T(8,128)(2,1)S(1)}, bf16[512,256]{1,0:T(8,128)(2,1)}, u32[]{:S(2)}) copy-start(bf16[512,256]{1,0:T(8,128)(2,1)} %constant.11.clone.basis) | copy-start | bytes 786436
  4.9 22.7 %copy-start.3 = (bf16[256,256]{1,0:T(8,128)(2,1)S(1)}, bf16[256,256]{1,0:T(8,128)(2,1)}, u32[]{:S(2)}) copy-start(bf16[256,256]{1,0:T(8,128)(2,1)} %constant.10.clone.perm) | copy-start | bytes 393220
  4.9 22.7 %copy-start.6 = (bf16[108,144]{1,0:T(8,128)(2,1)S(1)}, bf16[108,144]{1,0:T(8,128)(2,1)}, u32[]{:S(2)}) copy-start(bf16[108,144]{1,0:T(8,128)(2,1)} %constant.9.clone.kcol) | copy-start | bytes 93316
  4.9 18.4 %collective-permute-start = (bf16[16,1,257,128]{3,0,2,1:T(8,128)(2,1)S(1)}, bf16[16,1,257,128]{3,0,2,1:T(8,128)(2,1)S(1)}, u32[]{:S(2)}, u32[]{:S(2)}) collective-permute-start(bf16[16,1,257,128]{3,0,2,1:T(8,128)(2,1)S(1)} %copy.21), channel_id=1, source_target_pairs={{1,0},{2,1},{3,2},{4,3},{5,4},{6,5},{7,6},{9,8},{10,9},{11,10},{12... | collective-permute-start | bytes 3158024 | tf_op jit(solution)/shard_map/ppermute | solution.py:23
  9.4 18.1 %collective-permute-start.1 = (bf16[1,8,257,128]{3,1,2,0:T(8,128)(2,1)S(1)}, bf16[1,8,257,128]{3,1,2,0:T(8,128)(2,1)S(1)}, u32[]{:S(2)}, u32[]{:S(2)}) collective-permute-start(bf16[1,8,257,128]{3,1,2,0:T(8,128)(2,1)S(1)} %slice.10), channel_id=1, source_target_pairs={{8,0},{16,8},{24,16},{32,24},{40,32},{48,40},{56,48},{64,56},{72,6... | collective-permute-start | bytes 1579016 | tf_op jit(solution)/shard_map/ppermute | solution.py:23
  11.9 15.7 %collective-permute-start.2 = (bf16[1,1,257,128]{3,2,1,0:T(8,128)(2,1)S(1)}, bf16[1,1,257,128]{3,2,1,0:T(8,128)(2,1)S(1)}, u32[]{:S(2)}, u32[]{:S(2)}) collective-permute-start(bf16[1,1,257,128]{3,2,1,0:T(8,128)(2,1)S(1)} %copy.22), channel_id=1, source_target_pairs={{9,0},{10,1},{11,2},{12,3},{13,4},{14,5},{15,6},{17,8},{18,9},{19,... | collective-permute-start | bytes 197384 | tf_op jit(solution)/shard_map/ppermute | solution.py:33
  13.2 1.0 copy-start.1
  14.2 0.8 copy-start.9
  15.0 0.8 copy-start.10
  15.8 11.8 %copy-start.4 = (bf16[168,162]{1,0:T(8,128)(2,1)S(1)}, bf16[168,162]{1,0:T(8,128)(2,1)}, u32[]{:S(2)}) copy-start(bf16[168,162]{1,0:T(8,128)(2,1)} %constant.8.clone.qrow) | copy-start | bytes 163300
  15.8 11.9 %copy-start.7 = (bf16[162,108]{1,0:T(8,128)(2,1)S(1)}, bf16[162,108]{1,0:T(8,128)(2,1)}, u32[]{:S(2)}) copy-start(bf16[162,108]{1,0:T(8,128)(2,1)} %smap.1) | copy-start | bytes 104980
  63.8 42.6 %copy-start.8 = (f32[8192]{0:T(1024)S(1)}, f32[8192]{0:T(1024)}, u32[]{:S(2)}) copy-start(f32[8192]{0:T(1024)} %param.15) | copy-start | bytes 98308

commit v4 on v3

--- a/solution.py
+++ b/solution.py
@@ -52,7 +52,8 @@
     for i in range(3):
         for place, (j, k) in enumerate(places):
             for c in range(4):
-                cols[4 * (9 * i + 3 * j + k) + c, ROWS_K * i + 4 * place + c] = 1
+                row = 4 * place + (8 if place == 8 else 0)
+                cols[4 * (9 * i + 3 * j + k) + c, ROWS_K * i + row + c] = 1
     perm = np.zeros((256, 256), np.float32)
     for f in range(2):
         for d in range(16):
@@ -169,11 +170,12 @@
                 beyond, later = ordered(far(y + 2), far(y + 4))
             else:
                 beyond = later
-            at = b * ROWS_K
+            at = b * 32
             taps[slot, :, at : at + 16, :] = jnp.concatenate([before, middle], 1).astype(BF16)
             taps[slot, :, at + 16 : at + 32, :] = jnp.concatenate([after, held], 1).astype(BF16)
-            taps[slot, :, at + 32 : at + 48, :] = jnp.concatenate([beyond, beyond], 1).astype(BF16)
             before = after
+        last_tile = jnp.concatenate([beyond, beyond], 1).astype(BF16)
+        taps[slot, :, 32 * elem_rows + 16 : 32 * elem_rows + 32, :] = last_tile
 
     @pl.when(step > 0)
     def _():
@@ -196,13 +198,15 @@
         plane_slots = [lax.rem(2 * a + i, 3) for i in range(3)]
 
         def element_row(b, _):
-            at = pl.ds(pl.multiple_of(b * ROWS_K, 16), ROWS_K)
+            near = pl.ds(pl.multiple_of(b * 32, 16), 32)
+            next_far = pl.ds(pl.multiple_of(b * 32 + 48, 16), 16)
             scale = weight[a * elem_rows + b]
             pieces = []
             for d in range(16):
                 parts = [
                     jnp.concatenate([taps[s, d, at, :], taps[s, 16 + d, at, :]], 1)
                     for s in plane_slots
+                    for at in (near, next_far)
                 ]
                 strain = dot(mapped[...], jnp.concatenate(parts, 0))
                 product = strain[:, :128] * strain[:, 128:]
@@ -386,7 +390,7 @@
         scratch_shapes=[
             pltpu.VMEM((2, 2 * ODD_FROM, 128), F32),
             pltpu.VMEM((2, 264, 128), F32),
-            pltpu.VMEM((3, 32, 4 * ROWS_K, 128), BF16),
+            pltpu.VMEM((3, 32, 160, 128), BF16),
             pltpu.VMEM((ROWS_Q, 3 * ROWS_K), BF16),
             pltpu.VMEM((512, 512), BF16),
             pltpu.VMEM((512, 512), BF16),

time: 123 us -> 123 us (level)
  no operation moved by 1% of the time
where the time goes in v4:
time: 123 us; the launch traced here: 122 us
  Pallas kernels  59.8 us (49%)
  blocking collectives  42.6 us (35%)
  local copies, waits for them, and re-layouts  9.89 us (8%)
  starting transfers between devices  6.05 us (5%)
  waiting for transfers between devices  3.98 us (3%)
    all_to_all x1, blocking collectives, on_device(): lax.all_to_all(words.reshape(128, 33, 1, 128), AXES, split_axis=0, concat...  42.6 us
    pallas_call x1, Pallas kernels, on_device(): pl.pallas_call(partial_kernel, grid=(9,), out_shape=jax.ShapeDtypeStruct(...  36.2 us
    pallas_call x1, Pallas kernels, on_device(): pl.pallas_call(collect_kernel, out_shape=jax.ShapeDtypeStruct((128, cells...  16.1 us
    pallas_call x1, Pallas kernels, on_device(): pl.pallas_call(prepare_kernel, out_shape=(jax.ShapeDtypeStruct((elems //...  7.53 us
    ppermute x2, starting transfers between devices, shifted(): lax.ppermute(value, axis, [(source, source - 1) for source in range(1, co...  4.75 us
    slice x1, local copies, waits for them, and re-layouts, on_device(): side = shifted(fields[:, 0:1], 'cross')[:, 0]  4.63 us
    ppermute x1, waiting for transfers between devices, shifted_both(): return lax.ppermute(value, AXES, pairs)  3.98 us
    unnamed x26, local copies, waits for them, and re-layouts  2.8 us
  transfers between devices with their start and end apart: 3, of which 1 were waited for; matrix products, arithmetic and copies ran while one was open for 2% of the time, Pallas kernels for 6%

profile of v4, /device:TPU:1, one launch (start us, length us, event | category | flops | bytes accessed | tf_op | source)
XLA Modules:
  0.0 122.5 jit_solution(13261007721497786427)
XLA Ops:
  0.0 0.0 copy-start
  0.0 4.6 %slice.9 = bf16[16,1,257,128]{3,1,2,0:T(2,128)(2,1)S(1)} slice(bf16[16,8,257,128]{3,1,2,0:T(8,128)(2,1)} %param.12), slice={[0:16], [0:1], [0:257], [0:128]} | slice | bytes 2105344 | tf_op jit(solution)/shard_map/slice | solution.py:346
  4.6 0.0 copy-start.5
  4.6 0.0 copy-start.11
  4.7 0.2 copy.21
  4.8 0.0 copy-start.2
  4.9 0.0 copy-start.3
  4.9 0.0 copy-start.6
  4.9 3.5 %collective-permute-start = (bf16[16,1,257,128]{3,0,2,1:T(8,128)(2,1)S(1)}, bf16[16,1,257,128]{3,0,2,1:T(8,128)(2,1)S(1)}, u32[]{:S(2)}, u32[]{:S(2)}) collective-permute-start(bf16[16,1,257,128]{3,0,2,1:T(8,128)(2,1)S(1)} %copy.21), channel_id=1, source_target_pairs={{1,0},{2,1},{3,2},{4,3},{5,4},{6,5},{7,6},{9,8},{10,9},{11,10},{12... | collective-permute-start | bytes 3158024 | tf_op jit(solution)/shard_map/ppermute | solution.py:23
  8.4 1.1 slice.10
  9.4 1.3 %collective-permute-start.1 = (bf16[1,8,257,128]{3,1,2,0:T(8,128)(2,1)S(1)}, bf16[1,8,257,128]{3,1,2,0:T(8,128)(2,1)S(1)}, u32[]{:S(2)}, u32[]{:S(2)}) collective-permute-start(bf16[1,8,257,128]{3,1,2,0:T(8,128)(2,1)S(1)} %slice.10), channel_id=1, source_target_pairs={{8,0},{16,8},{24,16},{32,24},{40,32},{48,40},{56,48},{64,56},{72,6... | collective-permute-start | bytes 1579016 | tf_op jit(solution)/shard_map/ppermute | solution.py:23
  10.7 1.1 slice.11
  11.9 1.3 %collective-permute-start.2 = (bf16[1,1,257,128]{3,2,1,0:T(8,128)(2,1)S(1)}, bf16[1,1,257,128]{3,2,1,0:T(8,128)(2,1)S(1)}, u32[]{:S(2)}, u32[]{:S(2)}) collective-permute-start(bf16[1,1,257,128]{3,2,1,0:T(8,128)(2,1)S(1)} %copy.22), channel_id=1, source_target_pairs={{9,0},{10,1},{11,2},{12,3},{13,4},{14,5},{15,6},{17,8},{18,9},{19,... | collective-permute-start | bytes 197384 | tf_op jit(solution)/shard_map/ppermute | solution.py:33
  13.2 0.0 copy-done.5
  13.2 0.0 copy-done.11
  13.2 0.0 copy-start.1
  13.2 1.0 copy-done.1
  14.2 0.0 copy-start.9
  14.2 0.8 copy-done.9
  15.0 0.0 copy-start.10
  15.0 0.8 copy-done.10
  15.8 0.0 copy-start.4
  15.8 0.0 copy-start.7
  15.8 7.5 %shard_map.118 = (f32[32,32,128]{2,1,0:T(8,128)S(1)}, s32[32,128]{1,0:T(8,128)S(1)}, s32[32,128]{1,0:T(8,128)S(1)}) custom-call(s32[4096]{0:T(1024)S(1)} %copy-done.5, f32[27,4096]{1,0:T(8,128)S(1)} %copy-done.1, s32[32,128]{1,0:T(8,128)S(1)} %bitcast.27, s32[64,128]{1,0:T(8,128)S(1)} %bitcast.29, s32[1,128]{1,0:T(1,128)S(1)} %copy-done.11, ...), custom_call_target="tpu_custom_call" | custom-call | tf_op jit(solution)/shard_map/pallas_call | solution.py:353
  23.3 0.0 collective-permute-done
  23.3 0.3 copy.24
  23.6 4.0 %collective-permute-done.2 = bf16[1,1,257,128]{3,2,1,0:T(8,128)(2,1)S(1)} collective-permute-done((bf16[1,1,257,128]{3,2,1,0:T(8,128)(2,1)S(1)}, bf16[1,1,257,128]{3,2,1,0:T(8,128)(2,1)S(1)}, u32[]{:S(2)}, u32[]{:S(2)}) %collective-permute-start.2) | collective-permute-done | bytes 65824 | tf_op jit(solution)/shard_map/ppermute | solution.py:33
  27.6 0.0 collective-permute-done.1
  27.6 0.0 copy-done
  27.6 0.0 copy-done.2
  27.6 0.0 copy-done.3
  27.6 0.0 copy-done.6
  27.6 0.0 copy-done.4
  27.6 0.0 copy-done.7
  27.6 36.2 %shard_map.119 = s32[4224,128]{1,0:T(8,128)S(1)} custom-call(s32[32,128]{1,0:T(8,128)S(1)} %get-tuple-element.9.slots, bf16[16,257,8,128]{3,2,1,0:T(8,128)(2,1)S(1)} %bitcast.19, bf16[16,257,8,128]{3,2,1,0:T(8,128)(2,1)S(1)} %bitcast.20, bf16[16,257,128]{2,1,0:T(8,128)(2,1)S(1)} %bitcast.21, bf16[16,257,128]{2,1,0:T(8,128)(2,1)S(1)} %bitcast.22, ...), custom_call_target="tpu_custom_call" | custom-call | tf_op jit(solution)/shard_map/pallas_call | solution.py:370
  63.8 0.0 copy-start.8
  63.8 42.6 %all_to_all.5 = s32[128,33,1,128]{3,2,1,0:T(1,128)S(1)} all-to-all(s32[128,33,1,128]{3,2,1,0:T(1,128)S(1)} %bitcast.24), channel_id=1, replica_groups=mesh['slab'=16,'cross'=8] {'slab','cross'}, dimensions={0} | all-to-all | bytes 4325376 | tf_op jit(solution)/shard_map/all_to_all | solution.py:404
  106.4 0.0 copy-done.8
  106.4 16.1 %shard_map.120 = f32[128,8192]{1,0:T(8,128)} custom-call(s32[32,128]{1,0:T(8,128)S(1)} %get-tuple-element.8.cells, s32[4224,128]{1,0:T(8,128)S(1)} %bitcast.23, f32[64,128]{1,0:T(8,128)S(1)} %bitcast.28), custom_call_target="tpu_custom_call" | custom-call | tf_op jit(solution)/shard_map/pallas_call | solution.py:406
  (1 shorter events, 0.0 us)
Async XLA Ops:
  0.0 27.6 %copy-start = (bf16[16,8,257,128]{3,1,2,0:T(8,128)(2,1)S(1)}, bf16[16,8,257,128]{3,1,2,0:T(8,128)(2,1)}, u32[]{:S(2)}) copy-start(bf16[16,8,257,128]{3,1,2,0:T(8,128)(2,1)} %param.12) | copy-start | bytes 25264132
  4.6 8.5 %copy-start.5 = (s32[4096]{0:T(1024)S(1)}, s32[4096]{0:T(1024)}, u32[]{:S(2)}) copy-start(s32[4096]{0:T(1024)} %order_s.1) | copy-start | bytes 49156
  4.6 8.5 %copy-start.11 = (s32[1,128]{1,0:T(1,128)S(1)}, s32[1,128]{1,0:T(1,128)}, u32[]{:S(2)}) copy-start(s32[1,128]{1,0:T(1,128)} %count.1) | copy-start | bytes 1540
  4.8 22.7 %copy-start.2 = (bf16[512,256]{1,0:T(8,128)(2,1)S(1)}, bf16[512,256]{1,0:T(8,128)(2,1)}, u32[]{:S(2)}) copy-start(bf16[512,256]{1,0:T(8,128)(2,1)} %constant.11.clone.basis) | copy-start | bytes 786436
  4.9 22.7 %copy-start.3 = (bf16[256,256]{1,0:T(8,128)(2,1)S(1)}, bf16[256,256]{1,0:T(8,128)(2,1)}, u32[]{:S(2)}) copy-start(bf16[256,256]{1,0:T(8,128)(2,1)} %constant.10.clone.perm) | copy-start | bytes 393220
  4.9 22.7 %copy-start.6 = (bf16[108,144]{1,0:T(8,128)(2,1)S(1)}, bf16[108,144]{1,0:T(8,128)(2,1)}, u32[]{:S(2)}) copy-start(bf16[108,144]{1,0:T(8,128)(2,1)} %constant.9.clone.kcol) | copy-start | bytes 93316
  4.9 18.4 %collective-permute-start = (bf16[16,1,257,128]{3,0,2,1:T(8,128)(2,1)S(1)}, bf16[16,1,257,128]{3,0,2,1:T(8,128)(2,1)S(1)}, u32[]{:S(2)}, u32[]{:S(2)}) collective-permute-start(bf16[16,1,257,128]{3,0,2,1:T(8,128)(2,1)S(1)} %copy.21), channel_id=1, source_target_pairs={{1,0},{2,1},{3,2},{4,3},{5,4},{6,5},{7,6},{9,8},{10,9},{11,10},{12... | collective-permute-start | bytes 3158024 | tf_op jit(solution)/shard_map/ppermute | solution.py:23
  9.4 18.1 %collective-permute-start.1 = (bf16[1,8,257,128]{3,1,2,0:T(8,128)(2,1)S(1)}, bf16[1,8,257,128]{3,1,2,0:T(8,128)(2,1)S(1)}, u32[]{:S(2)}, u32[]{:S(2)}) collective-permute-start(bf16[1,8,257,128]{3,1,2,0:T(8,128)(2,1)S(1)} %slice.10), channel_id=1, source_target_pairs={{8,0},{16,8},{24,16},{32,24},{40,32},{48,40},{56,48},{64,56},{72,6... | collective-permute-start | bytes 1579016 | tf_op jit(solution)/shard_map/ppermute | solution.py:23
  11.9 15.7 %collective-permute-start.2 = (bf16[1,1,257,128]{3,2,1,0:T(8,128)(2,1)S(1)}, bf16[1,1,257,128]{3,2,1,0:T(8,128)(2,1)S(1)}, u32[]{:S(2)}, u32[]{:S(2)}) collective-permute-start(bf16[1,1,257,128]{3,2,1,0:T(8,128)(2,1)S(1)} %copy.22), channel_id=1, source_target_pairs={{9,0},{10,1},{11,2},{12,3},{13,4},{14,5},{15,6},{17,8},{18,9},{19,... | collective-permute-start | bytes 197384 | tf_op jit(solution)/shard_map/ppermute | solution.py:33
  13.2 1.0 copy-start.1
  14.2 0.8 copy-start.9
  15.0 0.8 copy-start.10
  15.8 11.8 %copy-start.4 = (bf16[168,162]{1,0:T(8,128)(2,1)S(1)}, bf16[168,162]{1,0:T(8,128)(2,1)}, u32[]{:S(2)}) copy-start(bf16[168,162]{1,0:T(8,128)(2,1)} %constant.8.clone.qrow) | copy-start | bytes 163300
  15.8 11.9 %copy-start.7 = (bf16[162,108]{1,0:T(8,128)(2,1)S(1)}, bf16[162,108]{1,0:T(8,128)(2,1)}, u32[]{:S(2)}) copy-start(bf16[162,108]{1,0:T(8,128)(2,1)} %smap.1) | copy-start | bytes 104980
  63.8 42.6 %copy-start.8 = (f32[8192]{0:T(1024)S(1)}, f32[8192]{0:T(1024)}, u32[]{:S(2)}) copy-start(f32[8192]{0:T(1024)} %param.15) | copy-start | bytes 98308
